TPU v7x, 128 devices: a whole 4x4x4 slice. The times are simulated.
128 devices in a mesh: expert: 16 (over z, y), tensor: 8 (over x, core).
Axes of the slice: x: 4, y: 4, z: 4, core: 2. Of those that a mesh axis runs over, the one named last changes fastest.
Arguments:
- tokens: bfloat16 [4096, 2048], P('expert', 'tensor'), may hold values from -6 to 6
- cotangent: bfloat16 [4096, 2048], P('expert', 'tensor'), may hold values from -6 to 6
- attn_gain: bfloat16 [2048], replicated, may hold values from 0.5 to 1.5
- w_query: bfloat16 [2048, 3072], P(None, 'tensor'), may hold values from -0.125 to 0.125
- w_latent: bfloat16 [2048, 576], replicated, may hold values from -0.125 to 0.125
- latent_gain: bfloat16 [512], replicated, may hold values from 0.5 to 1.5
- w_expand: bfloat16 [512, 4096], P(None, 'tensor'), may hold values from -0.25 to 0.25
- w_out: bfloat16 [2048, 2048], P('tensor'), may hold values from -0.5 to 0.5
- ffn_gain: bfloat16 [2048], replicated, may hold values from 0.5 to 1.5
- shared_gate: bfloat16 [2048, 2816], P(None, 'tensor'), may hold values from -0.125 to 0.125
- shared_up: bfloat16 [2048, 2816], P(None, 'tensor'), may hold values from -0.125 to 0.125
- shared_down: bfloat16 [2816, 2048], P('tensor'), may hold values from -0.109375 to 0.109375
- expert_gate: bfloat16 [64, 2048, 1408], P('expert', None, 'tensor'), may hold values from -0.125 to 0.125
- expert_up: bfloat16 [64, 2048, 1408], P('expert', None, 'tensor'), may hold values from -0.125 to 0.125
- expert_down: bfloat16 [64, 1408, 2048], P('expert', 'tensor'), may hold values from -0.21875 to 0.21875
- seq_lengths: int32 [64], replicated, may hold values from 1 to 253, as said below
- seq_order: int32 [64], replicated, may hold values from 0 to 63, as said below
- routes: int32 [4096, 6], P('expert'), may hold values from 0 to 63, all different within a row
- gate_weights: float32 [4096, 6], P('expert'), may hold values from 0.25 to 1
Outputs:
- output: bfloat16 [4096, 2048], P('expert', 'tensor')
- input_grad: bfloat16 [4096, 2048], P('expert', 'tensor')
- grad_attn_gain: float32 [2048], P('expert')
- grad_query: float32 [2048, 3072], P('expert', 'tensor')
- grad_latent: float32 [2048, 576], P('expert')
- grad_latent_gain: float32 [512], P('expert')
- grad_expand: float32 [512, 4096], P('expert', 'tensor')
- grad_out: float32 [2048, 2048], P('tensor', 'expert')
- feedforward_gain_gradient: float32 [2048], P('expert')
- grad_shared_gate: float32 [2048, 2816], P('expert', 'tensor')
- grad_shared_up: float32 [2048, 2816], P('expert', 'tensor')
- grad_shared_down: float32 [2816, 2048], P('tensor', 'expert')
- grad_expert_gate: float32 [64, 2048, 1408], P('expert', None, 'tensor')
- grad_expert_up: float32 [64, 2048, 1408], P('expert', None, 'tensor')
- grad_expert_down: float32 [64, 1408, 2048], P('expert', 'tensor')
Inputs may be any that keep to these rules, and one draw needn't show every extreme that they name: `seq_lengths`: in dealt order (sequence seq_order[j] at place j) every 4 consecutive places hold 256 tokens in all. `seq_order`: A permutation of the 64 sequences.
All inputs are finite; a program needn't handle non-finite values.
Results may differ from a plain program's by a relative error of at most 0.03.
Values may be sent and summed in bfloat16 or wider, within the bound.
A program may use at most 256 MiB of HBM per device.

v0:
```python
import jax
import jax.numpy as jnp
from jax import lax
from jax.sharding import PartitionSpec as P

NOPE = 128
ROPE = 64
LATENT = 512
VDIM = 128


EPS = 1e-06


def rms_scale(value, gain):
    return value * lax.rsqrt(jnp.mean(value * value, axis=-1, keepdims=True) + EPS) * gain


def rotate(value, offsets):
    half = value.shape[-1] // 2
    freqs = jnp.exp(-jnp.log(10000.0) * jnp.arange(half, dtype=jnp.float32) / half)
    angles = offsets.astype(jnp.float32)[:, None] * freqs[None, :]
    angles = angles.reshape((angles.shape[0],) + (1,) * (value.ndim - 2) + (half,))
    cosine = jnp.cos(angles)
    sine = jnp.sin(angles)
    first = value[..., :half]
    second = value[..., half:]
    return jnp.concatenate(
        [first * cosine - second * sine, second * cosine + first * sine], axis=-1
    )


def silu_product(gate_pre, up_pre):
    return gate_pre * jax.nn.sigmoid(gate_pre) * up_pre


def deal_layout(lengths, order, total):
    count = lengths.shape[0]
    begins = jnp.cumsum(lengths) - lengths
    dealt_lengths = lengths[order]
    dispatched_starts = jnp.cumsum(dealt_lengths) - dealt_lengths
    places = jnp.arange(total, dtype=jnp.int32)
    which = jnp.sum((places[:, None] >= dispatched_starts[None, :]).astype(jnp.int32), axis=1) - 1
    offsets = places - dispatched_starts[which]
    source = begins[order[which]] + offsets
    numbers = jnp.arange(count, dtype=jnp.int32)
    inverse_seq = jnp.sum(
        jnp.where(order[None, :] == numbers[:, None], numbers[None, :], 0), axis=1
    )
    owner = jnp.sum((places[:, None] >= begins[None, :]).astype(jnp.int32), axis=1) - 1
    target = dispatched_starts[inverse_seq[owner]] + places - begins[owner]
    return (source, target, offsets, which)


def product(left, right):
    return jnp.dot(left, right, preferred_element_type=jnp.float32)


def product_left(left, right):
    return lax.dot_general(
        left, right, (((0,), (0,)), ((), ())), preferred_element_type=jnp.float32
    )


def product_right(left, right):
    return lax.dot_general(
        left, right, (((1,), (1,)), ((), ())), preferred_element_type=jnp.float32
    )


def per_device(
    tokens,
    cotangent,
    attn_gain,
    w_query,
    w_latent,
    latent_gain,
    w_expand,
    w_out,
    ffn_gain,
    shared_gate,
    shared_up,
    shared_down,
    expert_gate,
    expert_up,
    expert_down,
    seq_lengths,
    seq_order,
    routes,
    gate_weights,
):
    token_groups = lax.axis_size("expert")
    group = lax.axis_index("expert")
    column = lax.axis_index("tensor")
    group_rows = tokens.shape[0]
    col_width = tokens.shape[1]
    model = col_width * lax.axis_size("tensor")
    total = group_rows * token_groups
    source, target, offsets, which = deal_layout(seq_lengths, seq_order, total)
    first_row = group * group_rows
    wanted = lax.dynamic_slice_in_dim(source, first_row, group_rows)
    local_offsets = lax.dynamic_slice_in_dim(offsets, first_row, group_rows)
    local_seqs = lax.dynamic_slice_in_dim(which, first_row, group_rows)
    blank = jnp.zeros((group_rows, col_width), jnp.bfloat16)
    pieces = (
        lax.all_gather(tokens, "expert", axis=0, tiled=True),
        lax.all_gather(cotangent, "expert", axis=0, tiled=True),
    )
    length = pieces[0].shape[0]
    shifted = wanted
    inside = (shifted >= 0) & (shifted < length)
    safe = jnp.clip(shifted, 0, length - 1)
    input_cols = jnp.where(inside[:, None], pieces[0][safe], blank)
    cotan_cols = jnp.where(inside[:, None], pieces[1][safe], blank)
    input_rows, output_grad = (
        lax.all_gather(input_cols, "tensor", axis=1, tiled=True),
        lax.all_gather(cotan_cols, "tensor", axis=1, tiled=True),
    )
    attn_gainf = attn_gain.astype(jnp.float32)
    ffn_gainf = ffn_gain.astype(jnp.float32)
    latent_gainf = latent_gain.astype(jnp.float32)
    dealt = input_rows.astype(jnp.float32)
    normed = rms_scale(dealt, attn_gainf).astype(jnp.bfloat16)
    head_width = NOPE + ROPE
    heads = w_query.shape[1] // head_width
    scale = head_width ** (-0.5)
    query_pre = product(normed, w_query).reshape(group_rows, heads, head_width)
    query = jnp.concatenate(
        [query_pre[..., :NOPE], rotate(query_pre[..., NOPE:], local_offsets)], axis=-1
    ).astype(jnp.bfloat16)
    latent = product(normed, w_latent)
    key_rope = rotate(latent[:, LATENT:], local_offsets).astype(jnp.bfloat16)
    latent_main = latent[:, :LATENT]
    compressed = rms_scale(latent_main, latent_gainf).astype(jnp.bfloat16)
    expanded = (
        product(compressed, w_expand).astype(jnp.bfloat16).reshape(group_rows, heads, NOPE + VDIM)
    )
    keys = jnp.concatenate(
        [expanded[..., :NOPE], jnp.broadcast_to(key_rope[:, None, :], (group_rows, heads, ROPE))],
        axis=-1,
    )
    values = expanded[..., NOPE:]
    places = jnp.arange(group_rows, dtype=jnp.int32)
    allowed = (local_seqs[:, None] == local_seqs[None, :]) & (places[:, None] >= places[None, :])

    def score_block():
        raw = jnp.einsum("qhd,khd->hqk", query, keys, preferred_element_type=jnp.float32) * scale
        return jnp.where(allowed[None], raw, -1e30)

    scores = score_block()
    peak = jnp.max(scores, axis=-1, keepdims=True)
    expo = jnp.exp(scores - peak)
    summed = jnp.sum(expo, axis=-1, keepdims=True)
    log_total = peak + jnp.log(summed)
    probs_low = (expo / summed).astype(jnp.bfloat16)
    mixed = jnp.einsum("hqk,khd->qhd", probs_low, values, preferred_element_type=jnp.float32)
    mixed = mixed.astype(jnp.bfloat16).reshape(group_rows, heads * VDIM)
    attn = lax.psum(product(mixed, w_out), "tensor")
    middle = dealt + attn
    normed_two = rms_scale(middle, ffn_gainf).astype(jnp.bfloat16)
    shared_g = product(normed_two, shared_gate)
    shared_u = product(normed_two, shared_up)
    shared_h = silu_product(shared_g, shared_u).astype(jnp.bfloat16)
    shared_part = product(shared_h, shared_down)
    local_experts = expert_gate.shape[0]
    experts = local_experts * token_groups
    top = routes.shape[1]
    capacity = (9 * group_rows * top + 8 * experts - 1) // (8 * experts)
    pair_expert = routes.reshape(-1)
    onehot = (pair_expert[:, None] == jnp.arange(experts, dtype=jnp.int32)[None, :]).astype(
        jnp.int32
    )
    slots = jnp.sum(onehot * jnp.cumsum(onehot, axis=0), axis=1) - 1
    kept = slots < capacity
    sentinel = experts * capacity
    place = jnp.where(kept, pair_expert * capacity + slots, sentinel)
    pair_token = jnp.arange(group_rows * top, dtype=jnp.int32) // top
    pair_gate = gate_weights.reshape(-1)
    match = place[:, None] == jnp.arange(sentinel, dtype=jnp.int32)[None, :]
    filled = jnp.any(match, axis=0)
    slot_token = jnp.sum(jnp.where(match, pair_token[:, None], 0), axis=0)
    slot_gate = jnp.sum(jnp.where(match, pair_gate[:, None], 0.0), axis=0)
    outgoing = jnp.where(filled[:, None], normed_two[slot_token], jnp.zeros((), jnp.bfloat16))
    outgoing = outgoing.reshape(token_groups, local_experts, capacity, model)
    received_rows = lax.all_to_all(outgoing, "expert", split_axis=0, concat_axis=0, tiled=True)
    gate_pre = jnp.einsum(
        "sekd,edh->sekh", received_rows, expert_gate, preferred_element_type=jnp.float32
    )
    up_pre = jnp.einsum(
        "sekd,edh->sekh", received_rows, expert_up, preferred_element_type=jnp.float32
    )
    hidden = silu_product(gate_pre, up_pre).astype(jnp.bfloat16)
    partial_value = jnp.einsum(
        "sekh,ehd->sekd", hidden, expert_down, preferred_element_type=jnp.float32
    )
    received_rows, partial_value, gate_pre, up_pre = (
        received_rows,
        partial_value.astype(jnp.bfloat16),
        gate_pre,
        up_pre,
    )
    returned = lax.all_to_all(
        partial_value, "expert", split_axis=0, concat_axis=0, tiled=True
    ).reshape(sentinel, model)
    returned = jnp.concatenate([returned, jnp.zeros((1, model), jnp.bfloat16)], axis=0)
    routed_part = jnp.sum(
        (pair_gate[:, None] * returned[place].astype(jnp.float32)).reshape(group_rows, top, model),
        axis=1,
    )
    moe_cols = lax.psum_scatter(
        (shared_part + routed_part).astype(jnp.bfloat16), "tensor", scatter_dimension=1, tiled=True
    ).astype(jnp.float32)
    output_cols = lax.dynamic_slice_in_dim(middle, column * col_width, col_width, 1) + moe_cols
    grad_dealt = output_grad.astype(jnp.float32)
    slot_grad = jnp.where(filled[:, None], slot_gate[:, None] * grad_dealt[slot_token], 0.0).astype(
        jnp.bfloat16
    )
    slot_grad = slot_grad.reshape(token_groups, local_experts, capacity, model)
    arrived_grad = lax.all_to_all(slot_grad, "expert", split_axis=0, concat_axis=0, tiled=True)
    hidden = silu_product(gate_pre, up_pre).astype(jnp.bfloat16)
    grad_edown = jnp.einsum(
        "sekh,sekd->ehd", hidden, arrived_grad, preferred_element_type=jnp.float32
    )
    grad_hidden = jnp.einsum(
        "sekd,ehd->sekh", arrived_grad, expert_down, preferred_element_type=jnp.float32
    )
    unused, silu_back = jax.vjp(silu_product, gate_pre, up_pre)
    grad_gpre, grad_upre = silu_back(grad_hidden)
    grad_glow = grad_gpre.astype(jnp.bfloat16)
    up_lowprec_gradient = grad_upre.astype(jnp.bfloat16)
    grad_egate = jnp.einsum(
        "ypwz,ypwj->pzj", received_rows, grad_glow, preferred_element_type=jnp.float32
    )
    expert_up_gradient = jnp.einsum(
        "ypwz,ypwj->pzj", received_rows, up_lowprec_gradient, preferred_element_type=jnp.float32
    )
    grad_rows = jnp.einsum(
        "sekh,edh->sekd", grad_glow, expert_gate, preferred_element_type=jnp.float32
    )
    grad_rows = grad_rows + jnp.einsum(
        "sekh,edh->sekd", up_lowprec_gradient, expert_up, preferred_element_type=jnp.float32
    )
    back_rows = lax.all_to_all(
        grad_rows.astype(jnp.bfloat16), "expert", split_axis=0, concat_axis=0, tiled=True
    ).reshape(sentinel, model)
    back_rows = jnp.concatenate([back_rows, jnp.zeros((1, model), jnp.bfloat16)], axis=0)
    routed_grad = jnp.sum(
        back_rows[place].astype(jnp.float32).reshape(group_rows, top, model), axis=1
    )
    grad_sdown = product_left(shared_h, output_grad)
    grad_sh = product_right(output_grad, shared_down)
    unused, shared_back = jax.vjp(silu_product, shared_g, shared_u)
    grad_sg, grad_su = shared_back(grad_sh)
    grad_sglow = grad_sg.astype(jnp.bfloat16)
    grad_sulow = grad_su.astype(jnp.bfloat16)
    grad_sgate = product_left(normed_two, grad_sglow)
    grad_sup = product_left(normed_two, grad_sulow)
    shared_grad = product_right(grad_sglow, shared_gate) + product_right(grad_sulow, shared_up)
    grad_normed_two = lax.psum((routed_grad + shared_grad).astype(jnp.bfloat16), "tensor").astype(
        jnp.float32
    )
    unused, norm_two_back = jax.vjp(rms_scale, middle, ffn_gainf)
    grad_mid_norm, grad_ffn = norm_two_back(grad_normed_two)
    grad_middle = grad_dealt + grad_mid_norm
    grad_attn = grad_middle.astype(jnp.bfloat16)
    grad_wout = product_left(mixed, grad_attn)
    grad_mixed = (
        product_right(grad_attn, w_out).astype(jnp.bfloat16).reshape(group_rows, heads, VDIM)
    )
    probs = jnp.exp(score_block() - log_total)
    grad_values = jnp.einsum(
        "hqk,qhd->khd", probs_low, grad_mixed, preferred_element_type=jnp.float32
    )
    grad_probs = jnp.einsum("qhd,khd->hqk", grad_mixed, values, preferred_element_type=jnp.float32)
    grad_scores = (
        probs * (grad_probs - jnp.sum(grad_probs * probs, axis=-1, keepdims=True))
    ).astype(jnp.bfloat16)
    grad_query = (
        jnp.einsum("hqk,khd->qhd", grad_scores, keys, preferred_element_type=jnp.float32) * scale
    )
    grad_keys = (
        jnp.einsum("hqk,qhd->khd", grad_scores, query, preferred_element_type=jnp.float32) * scale
    )
    unused, query_turn = jax.vjp(lambda part: rotate(part, local_offsets), query_pre[..., NOPE:])
    grad_qrot = query_turn(grad_query[..., NOPE:])[0]
    grad_qpre = jnp.concatenate([grad_query[..., :NOPE], grad_qrot], axis=-1)
    grad_qpre = grad_qpre.astype(jnp.bfloat16).reshape(group_rows, heads * head_width)
    rope_part = jnp.sum(grad_keys[..., NOPE:], axis=1)
    grad_expanded = jnp.concatenate([grad_keys[..., :NOPE], grad_values], axis=-1)
    grad_expanded = grad_expanded.astype(jnp.bfloat16).reshape(group_rows, heads * (NOPE + VDIM))
    grad_wexp = product_left(compressed, grad_expanded)
    compressed_part = product_right(grad_expanded, w_expand)
    grad_wq = product_left(normed, grad_qpre)
    normed_part = product_right(grad_qpre, w_query)
    normed_sum, compressed_sum, rope_sum = (
        lax.psum(normed_part.astype(jnp.bfloat16), "tensor").astype(jnp.float32),
        lax.psum(compressed_part.astype(jnp.bfloat16), "tensor").astype(jnp.float32),
        lax.psum(rope_part.astype(jnp.bfloat16), "tensor").astype(jnp.float32),
    )
    unused, latent_norm_back = jax.vjp(rms_scale, latent_main, latent_gainf)
    grad_lmain, grad_lgain = latent_norm_back(compressed_sum)
    unused, key_rotary_angles = jax.vjp(
        lambda part: rotate(part, local_offsets), latent[:, LATENT:]
    )
    grad_lrope = key_rotary_angles(rope_sum)[0]
    grad_latent_low = jnp.concatenate([grad_lmain, grad_lrope], axis=-1).astype(jnp.bfloat16)
    grad_wlat = product_left(normed, grad_latent_low)
    grad_normed = normed_sum + product_right(grad_latent_low, w_latent)
    unused, norm_one_back = jax.vjp(rms_scale, dealt, attn_gainf)
    grad_dealt_norm, grad_attn_g = norm_one_back(grad_normed)
    grad_input = grad_middle + grad_dealt_norm
    grad_cols_out = lax.dynamic_slice_in_dim(grad_input, column * col_width, col_width, 1)
    summed_grads = (
        lax.psum_scatter(
            grad_attn_g.astype(jnp.bfloat16), "expert", scatter_dimension=0, tiled=True
        ).astype(jnp.float32),
        lax.psum_scatter(
            grad_wq.astype(jnp.bfloat16), "expert", scatter_dimension=0, tiled=True
        ).astype(jnp.float32),
        lax.psum_scatter(
            grad_wlat.astype(jnp.bfloat16), "expert", scatter_dimension=0, tiled=True
        ).astype(jnp.float32),
        lax.psum_scatter(
            grad_lgain.astype(jnp.bfloat16), "expert", scatter_dimension=0, tiled=True
        ).astype(jnp.float32),
        lax.psum_scatter(
            grad_wexp.astype(jnp.bfloat16), "expert", scatter_dimension=0, tiled=True
        ).astype(jnp.float32),
        lax.psum_scatter(
            grad_wout.astype(jnp.bfloat16), "expert", scatter_dimension=1, tiled=True
        ).astype(jnp.float32),
        lax.psum_scatter(
            grad_ffn.astype(jnp.bfloat16), "expert", scatter_dimension=0, tiled=True
        ).astype(jnp.float32),
        lax.psum_scatter(
            grad_sgate.astype(jnp.bfloat16), "expert", scatter_dimension=0, tiled=True
        ).astype(jnp.float32),
        lax.psum_scatter(
            grad_sup.astype(jnp.bfloat16), "expert", scatter_dimension=0, tiled=True
        ).astype(jnp.float32),
        lax.psum_scatter(
            grad_sdown.astype(jnp.bfloat16), "expert", scatter_dimension=1, tiled=True
        ).astype(jnp.float32),
    )
    stacked = jnp.concatenate([output_cols, grad_cols_out], axis=1)
    stacked_lowprec = stacked.astype(jnp.bfloat16)
    local_target = lax.dynamic_slice_in_dim(target, first_row, group_rows)
    empty_rows = jnp.zeros((group_rows, 2 * col_width), jnp.bfloat16)
    piece = lax.all_gather(stacked_lowprec, "expert", axis=0, tiled=True)
    length = piece.shape[0]
    shifted = local_target
    inside = (shifted >= 0) & (shifted < length)
    safe = jnp.clip(shifted, 0, length - 1)
    final_low = jnp.where(inside[:, None], piece[safe], empty_rows)
    output_out = final_low[:, :col_width]
    grad_out_rows = final_low[:, col_width:]
    return (
        output_out,
        grad_out_rows,
        summed_grads[0],
        summed_grads[1],
        summed_grads[2],
        summed_grads[3],
        summed_grads[4],
        summed_grads[5],
        summed_grads[6],
        summed_grads[7],
        summed_grads[8],
        summed_grads[9],
        grad_egate,
        expert_up_gradient,
        grad_edown,
    )


def solution(mesh):
    return jax.shard_map(
        per_device,
        mesh=mesh,
        in_specs=(
            P("expert", "tensor"),
            P("expert", "tensor"),
            P(),
            P(None, "tensor"),
            P(),
            P(),
            P(None, "tensor"),
            P("tensor", None),
            P(),
            P(None, "tensor"),
            P(None, "tensor"),
            P("tensor", None),
            P("expert", None, "tensor"),
            P("expert", None, "tensor"),
            P("expert", "tensor", None),
            P(),
            P(),
            P("expert", None),
            P("expert", None),
        ),
        out_specs=(
            P("expert", "tensor"),
            P("expert", "tensor"),
            P("expert"),
            P("expert", "tensor"),
            P("expert", None),
            P("expert"),
            P("expert", "tensor"),
            P("tensor", "expert"),
            P("expert"),
            P("expert", "tensor"),
            P("expert", "tensor"),
            P("tensor", "expert"),
            P("expert", None, "tensor"),
            P("expert", None, "tensor"),
            P("expert", "tensor", None),
        ),
        check_vma=False,
    )
```

profile of v0, /device:TPU:1, one launch (start us, length us, event | category | flops | bytes accessed | tf_op | source)
XLA Modules:
  0.0 1622.9 jit_solution(8537835007125756969)
XLA Ops:
  30.3 5.1 compare_select_fusion.31
  43.6 36.6 %select_select_fusion.4 = s32[4096]{0:T(1024)S(1)} fusion(pred[4096]{0:T(1024)(128)(4,1)} %get-tuple-element.134, pred[4096]{0:T(1024)(128)(4,1)} %get-tuple-element.133, pred[4096]{0:T(1024)(128)(4,1)} %get-tuple-element.132, pred[4096]{0:T(1024)(128)(4,1)} %get-tuple-element.131, pred[4096]{0:T(1024)(128)(4,1)} %get-tuple-element.130, ...), kind=kLoop, calls=%fused_computation.462 | loop fusion | flops 233472 | bytes 266468 | tf_op jit(solution)/shard_map/gather | solution.py:51
  80.2 5.3 compare_select_fusion.10
  88.4 4.5 compare_select_fusion.18
  92.9 36.0 %select_select_fusion.1 = s32[4096]{0:T(1024)S(1)} fusion(pred[4096]{0:T(1024)(128)(4,1)S(1)} %get-tuple-element.248, pred[4096]{0:T(1024)(128)(4,1)S(1)} %get-tuple-element.247, pred[4096]{0:T(1024)(128)(4,1)S(1)} %get-tuple-element.246, pred[4096]{0:T(1024)(128)(4,1)S(1)} %get-tuple-element.245, pred[4096]{0:T(1024)(128)(4,1)S(1)} %get-tuple-element.244, ...), kind=kLoop, calls=%fused_computation.459 | loop fusion | flops 233472 | bytes 266468 | tf_op jit(solution)/shard_map/gather | solution.py:45
  128.9 4.6 compare_select_fusion.4
  136.6 32.5 %select_select_fusion = s32[4096]{0:T(1024)S(1)} fusion(pred[4096]{0:T(1024)(128)(4,1)S(1)} %get-tuple-element.187, pred[4096]{0:T(1024)(128)(4,1)S(1)} %get-tuple-element.186, pred[4096]{0:T(1024)(128)(4,1)S(1)} %get-tuple-element.136, pred[4096]{0:T(1024)(128)(4,1)S(1)} %get-tuple-element.137, pred[4096]{0:T(1024)(128)(4,1)S(1)} %get-tuple-element.138, ...), kind=kLoop, calls=%fused_computation.458 | loop fusion | flops 212992 | bytes 245968 | tf_op jit(solution)/shard_map/gather | solution.py:45
  169.2 36.0 %select_subtract_fusion = s32[4096]{0:T(1024)S(1)} fusion(pred[4096]{0:T(1024)(128)(4,1)S(1)} %get-tuple-element.248, pred[4096]{0:T(1024)(128)(4,1)S(1)} %get-tuple-element.247, pred[4096]{0:T(1024)(128)(4,1)S(1)} %get-tuple-element.246, pred[4096]{0:T(1024)(128)(4,1)S(1)} %get-tuple-element.245, pred[4096]{0:T(1024)(128)(4,1)S(1)} %get-tuple-element.244, ...), kind=kLoop, calls=%fused_computation.457 | loop fusion | flops 237568 | bytes 266468 | tf_op jit(solution)/shard_map/sub | solution.py:44
  216.8 31.5 %reduce-window.28 = s32[64,12,128]{2,1,0:T(8,128)S(1)} reduce-window(s32[64,12,128]{2,1,0:T(8,128)} %fusion.59, s32[]{:T(128)} %constant.28.clone.1), window={size=1x1x128 pad=0_0x0_0x127_0}, to_apply=%region_11.12 | reduce-window | flops 12484608 | bytes 786436 | tf_op jit(solution)/shard_map/reduce-window.2
  259.1 15.8 gather_fusion.5
  274.9 13.0 gather.65
  287.9 24.5 %fusion.1 = bf16[16,4,27,2048]{3,0,2,1:T(8,128)(2,1)} fusion(f32[16,4,27,2048]{3,2,1,0:T(8,128)} %gather.65, f32[16,4,27]{0,2,1:T(8,128)S(1)} %copy.156, pred[16,4,27]{0,2,1:T(8,128)(4,1)S(1)} %copy.147), kind=kLoop, calls=%fused_computation.12 | loop fusion | flops 10616832 | bytes 21242304 | tf_op jit(solution)/shard_map/convert_element_type | solution.py:215
  312.4 11.4 copy.158
  323.8 8.6 all-to-all-start.2
  351.2 67.2 %all-reduce.15.cloned.1.call-done = f32[256,2048]{1,0:T(8,128)} async-done(((f32[256,2048]{1,0:T(8,128)}), f32[256,2048]{1,0:T(8,128)}) %all-reduce.15.cloned.1.call-update) | async-done | bytes 2097168 | tf_op jit(solution)/shard_map/psum | solution.py:158
  423.1 15.9 gather_fusion.2
  439.0 9.6 gather.61
  448.6 14.5 copy_select_fusion
  463.1 11.6 copy.149
  474.6 6.6 all-to-all-start
  481.3 9.4 fusion.6
  490.7 89.8 %all-to-all-done = bf16[16,4,27,2048]{3,1,2,0:T(4,128)(2,1)} async-done(((bf16[16,4,27,2048]{3,1,2,0:T(4,128)(2,1)}), bf16[16,4,27,2048]{3,1,2,0:T(4,128)(2,1)}, u32[]{:S(2)}, u32[]{:S(2)}) %all-to-all-start) | async-done | bytes 7077920 | tf_op jit(solution)/shard_map/all_to_all | solution.py:185
  580.5 8.2 fusion.14
  588.8 9.8 fusion.44
  598.6 8.1 fusion.27
  606.6 11.4 fusion.3
  618.1 12.5 copy.160
  630.6 5.6 all-to-all-start.3
  636.2 6.8 convert_bitcast_fusion
  643.0 12.4 copy.152
  655.5 76.6 %all-to-all-done.3 = bf16[16,4,27,2048]{3,1,2,0:T(4,128)(2,1)} async-done(((bf16[16,4,27,2048]{3,1,2,0:T(4,128)(2,1)}), bf16[16,4,27,2048]{3,1,2,0:T(4,128)(2,1)}, u32[]{:S(2)}, u32[]{:S(2)}) %all-to-all-start.3) | async-done | bytes 7077920 | tf_op jit(solution)/shard_map/all_to_all | solution.py:243
  732.1 5.4 all-to-all-start.1
  745.6 11.1 copy.161
  756.7 9.7 reshape.484
  766.4 7.3 concatenate.41
  773.7 16.6 %gather_fusion.6 = bf16[1536,2048]{1,0:T(8,128)(2,1)} fusion(bf16[1729,2048]{1,0:T(8,128)(2,1)} %concatenate.41, s32[2048]{0:T(1024)S(1)} %pad_clamp_fusion), kind=kCustom, calls=%fused_computation.6 | custom fusion | bytes 12589056 | tf_op jit(solution)/shard_map/gather | solution.py:248
  790.3 11.7 reshape.487
  802.1 9.8 reduce_sum.198
  811.9 4.4 fusion.33
  816.4 12.1 all-to-all-done.1
  828.5 11.1 copy.153
  839.7 9.5 reshape.483
  849.2 7.3 concatenate.40
  856.5 16.7 %gather_fusion.3 = bf16[1536,2048]{1,0:T(8,128)(2,1)} fusion(bf16[1729,2048]{1,0:T(8,128)(2,1)} %concatenate.40, s32[2048]{0:T(1024)S(1)} %pad_clamp_fusion), kind=kCustom, calls=%fused_computation.3 | custom fusion | bytes 12589056 | tf_op jit(solution)/shard_map/gather | solution.py:207
  873.2 11.8 reshape.486
  885.0 13.7 all-reduce.17.cloned.1.call-done
  909.3 9.5 multiply_reduce_fusion
  942.3 40.9 %psum.39 = bf16[256,64]{0,1:T(8,128)(2,1)S(1)} all-reduce(bf16[256,64]{0,1:T(8,128)(2,1)S(1)} %slice_reduce_fusion), channel_id=1, replica_groups=mesh['expert'=16,'tensor'=8] {'tensor'}, use_global_device_ids=true, to_apply=%region_27.28 | all-reduce | flops 16384 | bytes 65536 | tf_op jit(solution)/shard_map/psum | solution.py:298
  983.5 6.7 all-reduce.19.cloned.1.call-done
  994.8 4.4 copy.185
  1005.1 17.9 %reduce-scatter.19.cloned.1.call-done = bf16[256,256]{1,0:T(8,128)(2,1)} async-done(((bf16[256,2048]{1,0:T(8,128)(2,1)}), bf16[256,256]{1,0:T(8,128)(2,1)}) %reduce-scatter.19.cloned.1.call-update) | async-done | bytes 131088 | tf_op jit(solution)/shard_map/reduce_scatter | solution.py:210
  1030.7 33.2 %select_select_fusion.2 = s32[4096]{0:T(1024)S(1)} fusion(pred[4096]{0:T(1024)(128)(4,1)} %get-tuple-element.129, pred[4096]{0:T(1024)(128)(4,1)S(1)} %copy-done.69, pred[4096]{0:T(1024)(128)(4,1)S(1)} %copy-done.71, pred[4096]{0:T(1024)(128)(4,1)S(1)} %copy-done.73, pred[4096]{0:T(1024)(128)(4,1)S(1)} %copy-done.75, pred[4096]{0:T(1024)(128)(4,1)S(1)} %copy-done.77, ...), kind=kLoop, calls=%fused_computation.460 | loop fusion | flops 212992 | bytes 245968 | tf_op jit(solution)/shard_map/gather | solution.py:51
  1063.9 33.5 %select_select_fusion.3 = s32[4096]{0:T(1024)S(1)} fusion(pred[4096]{0:T(1024)(128)(4,1)S(1)} %get-tuple-element.74, pred[4096]{0:T(1024)(128)(4,1)S(1)} %get-tuple-element.73, pred[4096]{0:T(1024)(128)(4,1)S(1)} %get-tuple-element.72, pred[4096]{0:T(1024)(128)(4,1)S(1)} %get-tuple-element.22, pred[4096]{0:T(1024)(128)(4,1)S(1)} %get-tuple-element.23, ...), kind=kLoop, calls=%fused_computation.461 | loop fusion | flops 217088 | bytes 250068 | tf_op jit(solution)/shard_map/gather | solution.py:51
  1097.4 6.2 compare_and_fusion.1
  1105.4 70.8 %reduce-scatter.31.cloned.1.call-done = bf16[128,352]{1,0:T(8,128)(2,1)} async-done(((bf16[2048,352]{1,0:T(8,128)(2,1)}), bf16[128,352]{1,0:T(8,128)(2,1)}) %reduce-scatter.31.cloned.1.call-update) | async-done | bytes 90128
  1177.9 74.6 %reduce-scatter.33.cloned.1.call-done = bf16[128,352]{1,0:T(8,128)(2,1)} async-done(((bf16[2048,352]{1,0:T(8,128)(2,1)}), bf16[128,352]{1,0:T(8,128)(2,1)}) %reduce-scatter.33.cloned.1.call-update) | async-done | bytes 90128
  1254.2 14.2 fusion.16
  1268.3 14.0 fusion.19
  1282.3 14.2 fusion.22
  1296.5 32.3 %all-reduce.9 = (bf16[2048]{0:T(1024)(128)(2,1)S(1)}, bf16[512]{0:T(512)(128)(2,1)S(1)}, bf16[2048]{0:T(1024)(128)(2,1)S(1)}) all-reduce(bf16[2048]{0:T(1024)(128)(2,1)S(1)} %get-tuple-element.17, bf16[512]{0:T(512)(128)(2,1)S(1)} %get-tuple-element.19, ...), channel_id=3, replica_groups=mesh['expert'=16,'tensor'=8] {'expert'}, use_global_device_ids=true, to_apply=%region_30.31.clone | all-reduce | flops 4608 | bytes 18432
  1332.0 71.0 %reduce-scatter.27.cloned.1.call-done = bf16[128,256]{1,0:T(8,128)(2,1)} async-done(((bf16[2048,256]{1,0:T(8,128)(2,1)}), bf16[128,256]{1,0:T(8,128)(2,1)}) %reduce-scatter.27.cloned.1.call-update) | async-done | bytes 65552
  1404.7 74.5 %reduce-scatter.21.cloned.1.call-done = bf16[128,384]{1,0:T(8,128)(2,1)} async-done(((bf16[2048,384]{1,0:T(8,128)(2,1)}), bf16[128,384]{1,0:T(8,128)(2,1)}) %reduce-scatter.21.cloned.1.call-update) | async-done | bytes 98320 | tf_op jit(solution)/shard_map/reduce_scatter | solution.py:317
  1480.9 75.9 %reduce-scatter.25.cloned.1.call-done = bf16[128,576]{1,0:T(8,128)(2,1)} async-done(((bf16[2048,576]{1,0:T(8,128)(2,1)}), bf16[128,576]{1,0:T(8,128)(2,1)}) %reduce-scatter.25.cloned.1.call-update) | async-done | bytes 147472
  1558.7 52.7 %all-gather.14.cloned.1.call-done = bf16[4096,512]{1,0:T(8,128)(2,1)} async-done(((bf16[256,512]{1,0:T(8,128)(2,1)}), bf16[4096,512]{1,0:T(8,128)(2,1)}) %all-gather.14.cloned.1.call-update) | async-done | bytes 4194320 | tf_op jit(solution)/shard_map/all_gather | solution.py:349
  (539 shorter events, 158.2 us)
Async XLA Ops:
  7.2 581.6 %copy-start = (bf16[4,2048,176]{1,2,0:T(8,128)(2,1)S(1)}, bf16[4,2048,176]{1,2,0:T(8,128)(2,1)}, u32[]{:S(2)}) copy-start(bf16[4,2048,176]{1,2,0:T(8,128)(2,1)} %param.32) | copy-start | bytes 8650756
  7.2 201.4 %all-gather.10.cloned.1.call-start = ((), (), s32[]{:S(2)}) async-start(), calls=%async_computation.16 | async-start | bytes 2228224 | tf_op jit(solution)/shard_map/all_gather | solution.py:107
  7.9 203.7 %all-gather.6.cloned.1.call-start = ((), (), s32[]{:S(2)}) async-start(), calls=%async_computation.12 | async-start | bytes 2228224 | tf_op jit(solution)/shard_map/all_gather | solution.py:106
  8.7 247.6 %all-gather.12.cloned.1.call-start = ((), (), s32[]{:S(2)}) async-start(), calls=%async_computation.17 | async-start | bytes 1179648 | tf_op jit(solution)/shard_map/all_gather | solution.py:117
  38.9 169.4 %copy-start.66 = (pred[4096]{0:T(1024)(128)(4,1)}, pred[4096]{0:T(1024)(128)(4,1)S(1)}, u32[]{:S(2)}) copy-start(pred[4096]{0:T(1024)(128)(4,1)S(1)} %get-tuple-element.78) | copy-start | bytes 12292
  38.9 169.4 %copy-start.68 = (pred[4096]{0:T(1024)(128)(4,1)}, pred[4096]{0:T(1024)(128)(4,1)S(1)}, u32[]{:S(2)}) copy-start(pred[4096]{0:T(1024)(128)(4,1)S(1)} %get-tuple-element.79) | copy-start | bytes 12292
  38.9 169.4 %copy-start.70 = (pred[4096]{0:T(1024)(128)(4,1)}, pred[4096]{0:T(1024)(128)(4,1)S(1)}, u32[]{:S(2)}) copy-start(pred[4096]{0:T(1024)(128)(4,1)S(1)} %get-tuple-element.80) | copy-start | bytes 12292
  39.0 169.5 %copy-start.72 = (pred[4096]{0:T(1024)(128)(4,1)}, pred[4096]{0:T(1024)(128)(4,1)S(1)}, u32[]{:S(2)}) copy-start(pred[4096]{0:T(1024)(128)(4,1)S(1)} %get-tuple-element.81) | copy-start | bytes 12292
  39.0 169.5 %copy-start.74 = (pred[4096]{0:T(1024)(128)(4,1)}, pred[4096]{0:T(1024)(128)(4,1)S(1)}, u32[]{:S(2)}) copy-start(pred[4096]{0:T(1024)(128)(4,1)S(1)} %get-tuple-element.82) | copy-start | bytes 12292
  39.0 169.5 %copy-start.76 = (pred[4096]{0:T(1024)(128)(4,1)}, pred[4096]{0:T(1024)(128)(4,1)S(1)}, u32[]{:S(2)}) copy-start(pred[4096]{0:T(1024)(128)(4,1)S(1)} %get-tuple-element.83) | copy-start | bytes 12292
  39.0 169.5 %copy-start.78 = (pred[4096]{0:T(1024)(128)(4,1)}, pred[4096]{0:T(1024)(128)(4,1)S(1)}, u32[]{:S(2)}) copy-start(pred[4096]{0:T(1024)(128)(4,1)S(1)} %get-tuple-element.84) | copy-start | bytes 12292
  39.0 169.5 %copy-start.80 = (pred[4096]{0:T(1024)(128)(4,1)}, pred[4096]{0:T(1024)(128)(4,1)S(1)}, u32[]{:S(2)}) copy-start(pred[4096]{0:T(1024)(128)(4,1)S(1)} %get-tuple-element.85) | copy-start | bytes 12292
  39.0 169.5 %copy-start.82 = (pred[4096]{0:T(1024)(128)(4,1)}, pred[4096]{0:T(1024)(128)(4,1)S(1)}, u32[]{:S(2)}) copy-start(pred[4096]{0:T(1024)(128)(4,1)S(1)} %get-tuple-element.86) | copy-start | bytes 12292
  39.0 169.5 %copy-start.84 = (pred[4096]{0:T(1024)(128)(4,1)}, pred[4096]{0:T(1024)(128)(4,1)S(1)}, u32[]{:S(2)}) copy-start(pred[4096]{0:T(1024)(128)(4,1)S(1)} %get-tuple-element.87) | copy-start | bytes 12292
  39.0 169.5 %copy-start.86 = (pred[4096]{0:T(1024)(128)(4,1)}, pred[4096]{0:T(1024)(128)(4,1)S(1)}, u32[]{:S(2)}) copy-start(pred[4096]{0:T(1024)(128)(4,1)S(1)} %get-tuple-element.88) | copy-start | bytes 12292
  39.0 169.5 %copy-start.88 = (pred[4096]{0:T(1024)(128)(4,1)}, pred[4096]{0:T(1024)(128)(4,1)S(1)}, u32[]{:S(2)}) copy-start(pred[4096]{0:T(1024)(128)(4,1)S(1)} %get-tuple-element.89) | copy-start | bytes 12292
  39.0 169.5 %copy-start.90 = (pred[4096]{0:T(1024)(128)(4,1)}, pred[4096]{0:T(1024)(128)(4,1)S(1)}, u32[]{:S(2)}) copy-start(pred[4096]{0:T(1024)(128)(4,1)S(1)} %get-tuple-element.90) | copy-start | bytes 12292
  39.0 169.5 %copy-start.92 = (pred[4096]{0:T(1024)(128)(4,1)}, pred[4096]{0:T(1024)(128)(4,1)S(1)}, u32[]{:S(2)}) copy-start(pred[4096]{0:T(1024)(128)(4,1)S(1)} %get-tuple-element.91) | copy-start | bytes 12292
  39.0 169.5 %copy-start.94 = (pred[4096]{0:T(1024)(128)(4,1)}, pred[4096]{0:T(1024)(128)(4,1)S(1)}, u32[]{:S(2)}) copy-start(pred[4096]{0:T(1024)(128)(4,1)S(1)} %get-tuple-element.92) | copy-start | bytes 12292
  39.1 169.5 %copy-start.96 = (pred[4096]{0:T(1024)(128)(4,1)}, pred[4096]{0:T(1024)(128)(4,1)S(1)}, u32[]{:S(2)}) copy-start(pred[4096]{0:T(1024)(128)(4,1)S(1)} %get-tuple-element.93) | copy-start | bytes 12292
  39.1 172.3 %copy-start.98 = (pred[4096]{0:T(1024)(128)(4,1)}, pred[4096]{0:T(1024)(128)(4,1)S(1)}, u32[]{:S(2)}) copy-start(pred[4096]{0:T(1024)(128)(4,1)S(1)} %get-tuple-element.94) | copy-start | bytes 12292
  39.1 172.3 %copy-start.100 = (pred[4096]{0:T(1024)(128)(4,1)}, pred[4096]{0:T(1024)(128)(4,1)S(1)}, u32[]{:S(2)}) copy-start(pred[4096]{0:T(1024)(128)(4,1)S(1)} %get-tuple-element.95) | copy-start | bytes 12292
  39.1 172.3 %copy-start.102 = (pred[4096]{0:T(1024)(128)(4,1)}, pred[4096]{0:T(1024)(128)(4,1)S(1)}, u32[]{:S(2)}) copy-start(pred[4096]{0:T(1024)(128)(4,1)S(1)} %get-tuple-element.96) | copy-start | bytes 12292
  39.1 172.3 %copy-start.104 = (pred[4096]{0:T(1024)(128)(4,1)}, pred[4096]{0:T(1024)(128)(4,1)S(1)}, u32[]{:S(2)}) copy-start(pred[4096]{0:T(1024)(128)(4,1)S(1)} %get-tuple-element.97) | copy-start | bytes 12292
  39.1 172.3 %copy-start.106 = (pred[4096]{0:T(1024)(128)(4,1)}, pred[4096]{0:T(1024)(128)(4,1)S(1)}, u32[]{:S(2)}) copy-start(pred[4096]{0:T(1024)(128)(4,1)S(1)} %get-tuple-element.98) | copy-start | bytes 12292
  39.1 172.3 %copy-start.108 = (pred[4096]{0:T(1024)(128)(4,1)}, pred[4096]{0:T(1024)(128)(4,1)S(1)}, u32[]{:S(2)}) copy-start(pred[4096]{0:T(1024)(128)(4,1)S(1)} %get-tuple-element.99) | copy-start | bytes 12292
  39.1 172.3 %copy-start.110 = (pred[4096]{0:T(1024)(128)(4,1)}, pred[4096]{0:T(1024)(128)(4,1)S(1)}, u32[]{:S(2)}) copy-start(pred[4096]{0:T(1024)(128)(4,1)S(1)} %get-tuple-element.100) | copy-start | bytes 12292
  39.1 172.3 %copy-start.112 = (pred[4096]{0:T(1024)(128)(4,1)}, pred[4096]{0:T(1024)(128)(4,1)S(1)}, u32[]{:S(2)}) copy-start(pred[4096]{0:T(1024)(128)(4,1)S(1)} %get-tuple-element.101) | copy-start | bytes 12292
  39.1 172.3 %copy-start.114 = (pred[4096]{0:T(1024)(128)(4,1)}, pred[4096]{0:T(1024)(128)(4,1)S(1)}, u32[]{:S(2)}) copy-start(pred[4096]{0:T(1024)(128)(4,1)S(1)} %get-tuple-element.102) | copy-start | bytes 12292
  39.2 172.3 %copy-start.116 = (pred[4096]{0:T(1024)(128)(4,1)}, pred[4096]{0:T(1024)(128)(4,1)S(1)}, u32[]{:S(2)}) copy-start(pred[4096]{0:T(1024)(128)(4,1)S(1)} %get-tuple-element.103) | copy-start | bytes 12292
  39.2 172.3 %copy-start.118 = (pred[4096]{0:T(1024)(128)(4,1)}, pred[4096]{0:T(1024)(128)(4,1)S(1)}, u32[]{:S(2)}) copy-start(pred[4096]{0:T(1024)(128)(4,1)S(1)} %get-tuple-element.104) | copy-start | bytes 12292
  39.2 172.3 %copy-start.120 = (pred[4096]{0:T(1024)(128)(4,1)}, pred[4096]{0:T(1024)(128)(4,1)S(1)}, u32[]{:S(2)}) copy-start(pred[4096]{0:T(1024)(128)(4,1)S(1)} %get-tuple-element.105) | copy-start | bytes 12292
  39.2 172.3 %copy-start.122 = (pred[4096]{0:T(1024)(128)(4,1)}, pred[4096]{0:T(1024)(128)(4,1)S(1)}, u32[]{:S(2)}) copy-start(pred[4096]{0:T(1024)(128)(4,1)S(1)} %get-tuple-element.106) | copy-start | bytes 12292
  39.2 172.3 %copy-start.124 = (pred[4096]{0:T(1024)(128)(4,1)}, pred[4096]{0:T(1024)(128)(4,1)S(1)}, u32[]{:S(2)}) copy-start(pred[4096]{0:T(1024)(128)(4,1)S(1)} %get-tuple-element.107) | copy-start | bytes 12292
  39.2 172.3 %copy-start.126 = (pred[4096]{0:T(1024)(128)(4,1)}, pred[4096]{0:T(1024)(128)(4,1)S(1)}, u32[]{:S(2)}) copy-start(pred[4096]{0:T(1024)(128)(4,1)S(1)} %get-tuple-element.108) | copy-start | bytes 12292
  39.2 172.3 %copy-start.128 = (pred[4096]{0:T(1024)(128)(4,1)}, pred[4096]{0:T(1024)(128)(4,1)S(1)}, u32[]{:S(2)}) copy-start(pred[4096]{0:T(1024)(128)(4,1)S(1)} %get-tuple-element.109) | copy-start | bytes 12292
  39.2 172.3 %copy-start.130 = (pred[4096]{0:T(1024)(128)(4,1)}, pred[4096]{0:T(1024)(128)(4,1)S(1)}, u32[]{:S(2)}) copy-start(pred[4096]{0:T(1024)(128)(4,1)S(1)} %get-tuple-element.110) | copy-start | bytes 12292
  39.2 172.3 %copy-start.132 = (pred[4096]{0:T(1024)(128)(4,1)}, pred[4096]{0:T(1024)(128)(4,1)S(1)}, u32[]{:S(2)}) copy-start(pred[4096]{0:T(1024)(128)(4,1)S(1)} %get-tuple-element.111) | copy-start | bytes 12292
  39.2 172.3 %copy-start.134 = (pred[4096]{0:T(1024)(128)(4,1)}, pred[4096]{0:T(1024)(128)(4,1)S(1)}, u32[]{:S(2)}) copy-start(pred[4096]{0:T(1024)(128)(4,1)S(1)} %get-tuple-element.112) | copy-start | bytes 12292
  39.3 172.3 %copy-start.136 = (pred[4096]{0:T(1024)(128)(4,1)}, pred[4096]{0:T(1024)(128)(4,1)S(1)}, u32[]{:S(2)}) copy-start(pred[4096]{0:T(1024)(128)(4,1)S(1)} %get-tuple-element.113) | copy-start | bytes 12292
  39.3 172.3 %copy-start.138 = (pred[4096]{0:T(1024)(128)(4,1)}, pred[4096]{0:T(1024)(128)(4,1)S(1)}, u32[]{:S(2)}) copy-start(pred[4096]{0:T(1024)(128)(4,1)S(1)} %get-tuple-element.114) | copy-start | bytes 12292
  39.3 172.3 %copy-start.139 = (pred[4096]{0:T(1024)(128)(4,1)}, pred[4096]{0:T(1024)(128)(4,1)S(1)}, u32[]{:S(2)}) copy-start(pred[4096]{0:T(1024)(128)(4,1)S(1)} %get-tuple-element.115) | copy-start | bytes 12292
  39.3 172.3 %copy-start.140 = (pred[4096]{0:T(1024)(128)(4,1)}, pred[4096]{0:T(1024)(128)(4,1)S(1)}, u32[]{:S(2)}) copy-start(pred[4096]{0:T(1024)(128)(4,1)S(1)} %get-tuple-element.116) | copy-start | bytes 12292
  215.3 117.9 %all-gather.8.cloned.1.call-start = ((), (), s32[]{:S(2)}) async-start(), calls=%async_computation.13 | async-start | bytes 1179648 | tf_op jit(solution)/shard_map/all_gather | solution.py:116
  215.9 127.6 %copy-start.52 = (f32[2048]{0:T(1024)}, f32[2048]{0:T(1024)S(1)}, u32[]{:S(2)}) copy-start(f32[2048]{0:T(1024)S(1)} %convert_element_type.222) | copy-start | bytes 24580
  215.9 123.1 %copy-start.62 = (f32[512]{0:T(512)}, f32[512]{0:T(512)S(1)}, u32[]{:S(2)}) copy-start(f32[512]{0:T(512)S(1)} %convert_element_type.224) | copy-start | bytes 6148
  323.8 150.9 %all-to-all-start.2 = ((bf16[16,4,27,2048]{3,1,2,0:T(4,128)(2,1)}), bf16[16,4,27,2048]{3,1,2,0:T(4,128)(2,1)}, u32[]{:S(2)}, u32[]{:S(2)}) async-start(bf16[16,4,27,2048]{3,1,2,0:T(4,128)(2,1)} %copy.158), calls=%async_computation.3 | async-start | bytes 14155776 | tf_op jit(solution)/shard_map/all_to_all | solution.py:219
  332.4 85.9 %all-reduce.15.cloned.1.call-start = ((), (), s32[]{:S(2)}) async-start(), calls=%async_computation.14 | async-start | bytes 4194304 | tf_op jit(solution)/shard_map/psum | solution.py:158
  474.6 105.9 %all-to-all-start = ((bf16[16,4,27,2048]{3,1,2,0:T(4,128)(2,1)}), bf16[16,4,27,2048]{3,1,2,0:T(4,128)(2,1)}, u32[]{:S(2)}, u32[]{:S(2)}) async-start(bf16[16,4,27,2048]{3,1,2,0:T(4,128)(2,1)} %copy.149), calls=%async_computation | async-start | bytes 14155776 | tf_op jit(solution)/shard_map/all_to_all | solution.py:185
  630.6 101.5 %all-to-all-start.3 = ((bf16[16,4,27,2048]{3,1,2,0:T(4,128)(2,1)}), bf16[16,4,27,2048]{3,1,2,0:T(4,128)(2,1)}, u32[]{:S(2)}, u32[]{:S(2)}) async-start(bf16[16,4,27,2048]{3,1,2,0:T(4,128)(2,1)} %copy.160), calls=%async_computation.4 | async-start | bytes 14155776 | tf_op jit(solution)/shard_map/all_to_all | solution.py:243
  732.1 96.4 %all-to-all-start.1 = ((bf16[16,4,27,2048]{3,1,2,0:T(4,128)(2,1)}), bf16[16,4,27,2048]{3,1,2,0:T(4,128)(2,1)}, u32[]{:S(2)}, u32[]{:S(2)}) async-start(bf16[16,4,27,2048]{3,1,2,0:T(4,128)(2,1)} %copy.152), calls=%async_computation.1 | async-start | bytes 14155776 | tf_op jit(solution)/shard_map/all_to_all | solution.py:202
  737.5 161.2 %all-reduce.17.cloned.1.call-start = ((), (), s32[]{:S(2)}) async-start(), calls=%async_computation.18 | async-start | bytes 2097152 | tf_op jit(solution)/shard_map/psum | solution.py:259
  816.3 173.8 %all-reduce.19.cloned.1.call-start = ((), (), s32[]{:S(2)}) async-start(), calls=%async_computation.27 | async-start | bytes 2621440 | tf_op jit(solution)/shard_map/psum | solution.py:296
  909.2 113.8 %reduce-scatter.19.cloned.1.call-start = ((), (), s32[]{:S(2)}) async-start(), calls=%async_computation.15 | async-start | bytes 1179648 | tf_op jit(solution)/shard_map/reduce_scatter | solution.py:210
  920.6 183.1 %reduce-scatter.29.cloned.1.call-start = ((), (), s32[]{:S(2)}) async-start(), calls=%async_computation.24 | async-start | bytes 1671168
  924.9 251.3 %reduce-scatter.31.cloned.1.call-start = ((), (), s32[]{:S(2)}) async-start(), calls=%async_computation.25 | async-start | bytes 1671168
  929.2 323.2 %reduce-scatter.33.cloned.1.call-start = ((), (), s32[]{:S(2)}) async-start(), calls=%async_computation.26 | async-start | bytes 1671168
  933.6 397.0 %reduce-scatter.23.cloned.1.call-start = ((), (), s32[]{:S(2)}) async-start(), calls=%async_computation.21 | async-start | bytes 557056 | tf_op jit(solution)/shard_map/reduce_scatter | solution.py:326
  934.9 468.2 %reduce-scatter.27.cloned.1.call-start = ((), (), s32[]{:S(2)}) async-start(), calls=%async_computation.23 | async-start | bytes 1114112
  939.2 540.0 %reduce-scatter.21.cloned.1.call-start = ((), (), s32[]{:S(2)}) async-start(), calls=%async_computation.20 | async-start | bytes 1671168 | tf_op jit(solution)/shard_map/reduce_scatter | solution.py:317
  941.3 615.6 %reduce-scatter.25.cloned.1.call-start = ((), (), s32[]{:S(2)}) async-start(), calls=%async_computation.22 | async-start | bytes 2785280
  999.2 612.1 %all-gather.14.cloned.1.call-start = ((), (), s32[]{:S(2)}) async-start(), calls=%async_computation.19 | async-start | bytes 4456448 | tf_op jit(solution)/shard_map/all_gather | solution.py:349
  1003.9 250.2 %copy-start.21 = (bf16[16,4,27,176]{3,2,0,1:T(8,128)(2,1)S(1)}, bf16[16,4,27,176]{3,2,0,1:T(8,128)(2,1)}, u32[]{:S(2)}) copy-start(bf16[16,4,27,176]{3,2,0,1:T(8,128)(2,1)} %copy-done.20) | copy-start | bytes 1824772
  1479.2 136.9 %copy-start.1 = (bf16[4,2048,176]{1,2,0:T(8,128)(2,1)S(1)}, bf16[4,2048,176]{1,2,0:T(8,128)(2,1)}, u32[]{:S(2)}) copy-start(bf16[4,2048,176]{1,2,0:T(8,128)(2,1)} %param.32) | copy-start | bytes 8650756
  (122 other events, 2330.6 us)
Sparse Core Ops, SparseCore 0:
  10.2 47.4 all-gather.9
  59.8 44.5 all-gather.5
  215.4 26.9 all-gather.11
  255.2 26.9 all-gather.7
  351.3 67.0 all-reduce.14
  816.4 82.2 all-reduce.16
  909.4 80.7 all-reduce.18
  992.5 30.4 reduce-scatter.18
  1026.3 73.8 reduce-scatter.28
  1103.2 72.9 reduce-scatter.30
  1179.4 72.9 reduce-scatter.32
  1255.5 71.6 reduce-scatter.22
  1330.7 72.3 reduce-scatter.26
  1406.1 73.0 reduce-scatter.20
  1482.3 74.4 reduce-scatter.24
  1558.9 52.4 all-gather.13
where the time goes:
time: 1640 us; the launch traced here: 1620 us
  waiting for transfers between devices  705 us (43%)
  other arithmetic  381 us (23%)
  local copies, waits for them, and re-layouts  282 us (17%)
  matrix products  135 us (8%)
  blocking collectives  73.3 us (4%)
  starting transfers between devices  27.5 us (2%)
  between operations  18.2 us (1%)
    unnamed x21, waiting for transfers between devices  294 us
    gather x8, other arithmetic, deal_layout(): target = dispatched_starts[inverse_seq[owner]] + places - begins[owner]  124 us
    all_to_all x1, waiting for transfers between devices, per_device(): lax.all_to_all(outgoing, 'expert', split_axis=0, concat_axis=0, tiled=True)  89.8 us
    gather x6, other arithmetic, deal_layout(): source = begins[order[which]] + offsets  83.6 us
    all_to_all x1, waiting for transfers between devices, per_device(): lax.all_to_all(grad_rows.astype(jnp.bfloat16), 'expert', split_axis=0, co...  76.6 us
    reduce_scatter x1, waiting for transfers between devices, per_device(): lax.psum_scatter(grad_wq.astype(jnp.bfloat16), 'expert', scatter_dimensio...  74.5 us
    psum x1, waiting for transfers between devices, per_device(): attn = lax.psum(product(mixed, w_out), 'tensor')  67.2 us
    all_gather x1, waiting for transfers between devices, per_device(): piece = lax.all_gather(stacked_lowprec, 'expert', axis=0, tiled=True)  52.7 us
  transfers between devices with their start and end apart: 20, of which 13 were waited for; matrix products, arithmetic and copies ran while one was open for 44% of the time, Pallas kernels for 0%

commit v1 on v0

v1 whole, which is shorter than its diff:
```python
import functools

import jax
import jax.numpy as jnp
from jax import lax
from jax.experimental import pallas as pl
from jax.experimental.pallas import tpu as pltpu
from jax.sharding import PartitionSpec as P

NOPE = 128
ROPE = 64
HEAD = NOPE + ROPE
LATENT = 512
VDIM = 128
D = 2048
GROUP = 256
TOP = 6
EXPERTS = 64
GROUPS = 16
LOCAL = 4
CAP = 27
PADCAP = 32
TENSOR = 8
COLS = D // TENSOR
EPS = 1e-06

XN = 4
YN = 4
ZN = 4
CORES = 2

F32 = jnp.float32
BF16 = jnp.bfloat16
MESH = pl.DeviceIdType.MESH
ANY = pl.BlockSpec(memory_space=pl.ANY)
VM = pl.BlockSpec(memory_space=pltpu.VMEM)
DMA = pltpu.SemaphoreType.DMA
MIB = 1024 * 1024


def remote(src, dst, ssem, rsem, axis, index):
    return pltpu.make_async_remote_copy(
        src_ref=src,
        dst_ref=dst,
        send_sem=ssem,
        recv_sem=rsem,
        device_id={axis: index},
        device_id_type=MESH,
    )


def greet(peers):
    barrier = pltpu.get_barrier_semaphore()
    for axis, index in peers:
        pl.semaphore_signal(barrier, inc=1, device_id={axis: index}, device_id_type=MESH)
    pl.semaphore_wait(barrier, len(peers))


def params(cid, vmem=48):
    return pltpu.CompilerParams(
        collective_id=cid, has_side_effects=True, vmem_limit_bytes=vmem * MIB
    )


def x_peers():
    t = lax.axis_index("tensor")
    x = t // CORES
    c = lax.rem(t, CORES)
    right = lax.rem(x + 1, XN) * CORES + c
    left = lax.rem(x + XN - 1, XN) * CORES + c
    far = lax.rem(x + 2, XN) * CORES + c
    twin = x * CORES + (1 - c)
    return t, right, left, far, twin


def greet_x():
    t, right, left, far, twin = x_peers()
    greet([("tensor", right), ("tensor", left), ("tensor", twin)])


def greet_tensor():
    t = lax.axis_index("tensor")
    greet([("tensor", lax.rem(t + j, TENSOR)) for j in range(1, TENSOR)])


def cols(index, width):
    return pl.ds(pl.multiple_of(index * width, width), width)


def gather_tensor(nch, src, out_ref, ssem, rsem):
    t, right, left, far, twin = x_peers()
    flip = twin - t
    rows, width = src.shape
    rc = rows // nch
    h = rc // 2

    def block(k, owner, part=None):
        if part is None:
            return out_ref.at[pl.ds(k * rc, rc), cols(owner, width)]
        return out_ref.at[pl.ds(k * rc + part * h, h), cols(owner, width)]

    sends = []

    def send(k, j, ref, dst, target):
        c = remote(ref, dst, ssem.at[k, j], rsem.at[k, j], "tensor", target)
        c.start()
        sends.append(c)

    def arrived(k, j, ref):
        remote(ref, ref, ssem.at[k, j], rsem.at[k, j], "tensor", twin).wait_recv()

    for k in range(nch):
        part = src.at[pl.ds(k * rc, rc), :]
        send(k, 0, part, block(k, t), right)
        send(k, 1, part, block(k, t), left)
        send(k, 4, part, block(k, t), twin)
    for k in range(nch):
        arrived(k, 0, block(k, left))
        send(k, 2, block(k, left, 0), block(k, left, 0), right)
        send(k, 5, block(k, left), block(k, left), twin)
        arrived(k, 1, block(k, right))
        send(k, 3, block(k, right, 1), block(k, right, 1), left)
        send(k, 6, block(k, right), block(k, right), twin)
    for k in range(nch):
        arrived(k, 2, block(k, far, 0))
        send(k, 7, block(k, far, 0), block(k, far, 0), twin)
        arrived(k, 3, block(k, far, 1))
        send(k, 8, block(k, far, 1), block(k, far, 1), twin)
    for k in range(nch):
        arrived(k, 4, block(k, twin))
        arrived(k, 5, block(k, left + flip))
        arrived(k, 6, block(k, right + flip))
        arrived(k, 7, block(k, far + flip, 0))
        arrived(k, 8, block(k, far + flip, 1))
    for s in sends:
        s.wait_send()


def gather_sems(nch):
    return [DMA((nch, 9)), DMA((nch, 9))]


def scatter_tensor(nch, view, rows, width, emit, own, sib, half, full, ssem, rsem, lsem):
    t, right, left, far, twin = x_peers()
    flip = twin - t
    rc = rows // nch
    h = rc // 2
    order = (far, right, left, t)
    sends = []

    def send(k, j, src, dst, target):
        c = remote(src, dst, ssem.at[k, j], rsem.at[k, j], "tensor", target)
        c.start()
        sends.append(c)

    def arrived(k, j, ref):
        remote(ref, ref, ssem.at[k, j], rsem.at[k, j], "tensor", twin).wait_recv()

    loads = {}
    for k in range(nch):
        r = pl.ds(k * rc, rc)
        for j, owner in enumerate(order):
            send(k, j, view(r, owner + flip), sib.at[j, r], twin)
            c = pltpu.make_async_copy(view(r, owner), own.at[j, r], lsem.at[k, j])
            c.start()
            loads[k, j] = c

    def pair(k, j):
        loads[k, j].wait()
        arrived(k, j, sib.at[j, pl.ds(k * rc, rc)])

    def add(j, r):
        return own[j, r].astype(F32) + sib[j, r].astype(F32)

    for k in range(nch):
        r0, r1 = pl.ds(k * rc, h), pl.ds(k * rc + h, h)
        r, hk = pl.ds(k * rc, rc), pl.ds(k * h, h)
        pair(k, 0)
        own[0, r] = add(0, r).astype(own.dtype)
        send(k, 4, own.at[0, r0], half.at[0, hk], right)
        send(k, 5, own.at[0, r1], half.at[1, hk], left)
    for k in range(nch):
        r0, r1 = pl.ds(k * rc, h), pl.ds(k * rc + h, h)
        r, hk = pl.ds(k * rc, rc), pl.ds(k * h, h)
        pair(k, 1)
        pair(k, 2)
        arrived(k, 4, half.at[0, hk])
        own[1, r1] = add(1, r1).astype(own.dtype)
        own[1, r0] = (add(1, r0) + half[0, hk].astype(F32)).astype(own.dtype)
        send(k, 6, own.at[1, r], full.at[0, r], right)
        arrived(k, 5, half.at[1, hk])
        own[2, r0] = add(2, r0).astype(own.dtype)
        own[2, r1] = (add(2, r1) + half[1, hk].astype(F32)).astype(own.dtype)
        send(k, 7, own.at[2, r], full.at[1, r], left)
    for k in range(nch):
        r = pl.ds(k * rc, rc)
        pair(k, 3)
        arrived(k, 6, full.at[0, r])
        arrived(k, 7, full.at[1, r])
        emit(r, add(3, r) + full[0, r].astype(F32) + full[1, r].astype(F32))
    for s in sends:
        s.wait_send()


def scatter_scratch(nch, rows, width, dtype):
    return [
        pltpu.VMEM((4, rows, width), dtype),
        pltpu.VMEM((4, rows, width), dtype),
        pltpu.VMEM((2, rows // 2, width), dtype),
        pltpu.VMEM((2, rows, width), dtype),
        DMA((nch, 8)),
        DMA((nch, 8)),
        DMA((nch, 4)),
    ]


def sum_rows_tensor(value, buf, ssem, rsem):
    t = lax.axis_index("tensor")
    rows = value.shape[0]
    mine = jnp.broadcast_to(jnp.sum(value, axis=1, keepdims=True), (rows, 128))
    buf[t] = jnp.transpose(mine)[:8]
    sends = []
    for j in range(1, TENSOR):
        to = lax.rem(t + j, TENSOR)
        c = remote(buf.at[t], buf.at[t], ssem.at[j], rsem.at[j], "tensor", to)
        c.start()
        sends.append(c)
    for j in range(1, TENSOR):
        ref = buf.at[lax.rem(t + TENSOR - j, TENSOR)]
        remote(ref, ref, ssem.at[j], rsem.at[j], "tensor", t).wait_recv()
    total = jnp.sum(buf[...], axis=0)
    for s in sends:
        s.wait_send()
    return jnp.transpose(total)[:, :1]


def sum_rows_scratch():
    return [pltpu.VMEM((TENSOR, 8, GROUP), F32), DMA((TENSOR,)), DMA((TENSOR,))]


def ag_tensor_kernel(nch, in_ref, out_ref, ssem, rsem, lsem):
    t = lax.axis_index("tensor")
    greet_x()
    own = pltpu.make_async_copy(in_ref, out_ref.at[:, cols(t, in_ref.shape[1])], lsem)
    own.start()
    gather_tensor(nch, in_ref, out_ref, ssem, rsem)
    own.wait()


def ag_tensor(value, cid, nch=1):
    rows, width = value.shape
    return pl.pallas_call(
        functools.partial(ag_tensor_kernel, nch),
        out_shape=jax.ShapeDtypeStruct((rows, width * TENSOR), value.dtype),
        in_specs=[ANY],
        out_specs=ANY,
        scratch_shapes=gather_sems(nch) + [DMA],
        compiler_params=params(cid),
        name="ag_tensor",
    )(value)


def rs_tensor_kernel(nch, in_ref, out_ref, *scratch):
    rows = in_ref.shape[0]
    width = in_ref.shape[1] // TENSOR
    greet_x()

    def emit(r, value):
        out_ref[r] = value.astype(out_ref.dtype)

    scatter_tensor(
        nch, lambda r, owner: in_ref.at[r, cols(owner, width)], rows, width, emit, *scratch
    )


def rs_tensor(value, cid, nch=1, dtype=None):
    rows, total = value.shape
    width = total // TENSOR
    return pl.pallas_call(
        functools.partial(rs_tensor_kernel, nch),
        out_shape=jax.ShapeDtypeStruct((rows, width), dtype or value.dtype),
        in_specs=[ANY],
        out_specs=VM,
        scratch_shapes=scatter_scratch(nch, rows, width, value.dtype),
        compiler_params=params(cid),
        name="rs_tensor",
    )(value)


def middle_kernel(
    part_ref, x_ref, gain_ref, mid_ref, inv_ref, low_ref, full_ref, *scratch
):
    rs, ag, st, lsem = scratch[:7], scratch[7:9], scratch[9:12], scratch[12]
    t = lax.axis_index("tensor")
    greet_tensor()

    def emit(r, value):
        mid_ref[r] = x_ref[r].astype(F32) + value

    scatter_tensor(1, lambda r, owner: part_ref.at[r, cols(owner, COLS)], GROUP, COLS, emit, *rs)
    mid = mid_ref[...]
    inv = lax.rsqrt(sum_rows_tensor(mid * mid, *st) * (1.0 / D) + EPS)
    inv_ref[...] = inv
    low_ref[...] = (mid * inv * gain_ref[...].astype(F32)).astype(BF16)
    own = pltpu.make_async_copy(low_ref, full_ref.at[:, cols(t, COLS)], lsem)
    own.start()
    gather_tensor(1, low_ref, full_ref, *ag)
    own.wait()


def middle_step(part, x_cols, gain, cid):
    return pl.pallas_call(
        middle_kernel,
        out_shape=(
            jax.ShapeDtypeStruct((GROUP, COLS), F32),
            jax.ShapeDtypeStruct((GROUP, 1), F32),
            jax.ShapeDtypeStruct((GROUP, COLS), BF16),
            jax.ShapeDtypeStruct((GROUP, D), BF16),
        ),
        in_specs=[ANY, VM, VM],
        out_specs=(VM, VM, VM, ANY),
        scratch_shapes=scatter_scratch(1, GROUP, COLS, F32)
        + gather_sems(1)
        + sum_rows_scratch()
        + [DMA],
        compiler_params=params(cid),
        name="middle_step",
    )(part, x_cols, gain)


def back_middle_kernel(
    routed_ref, shared_ref, mid_ref, inv_ref, gain_ref, dy_ref,
    dmid_ref, dgain_ref, full_ref, low, buf, ssem, rsem, agss, agrs, lsem
):
    t = lax.axis_index("tensor")
    greet_tensor()
    dn = routed_ref[...] + shared_ref[...]
    mid = mid_ref[...]
    inv = inv_ref[...]
    u = dn * gain_ref[...].astype(F32)
    total = sum_rows_tensor(u * mid, buf, ssem, rsem)
    dmid = dy_ref[...].astype(F32) + inv * u - mid * (inv * inv * inv * total * (1.0 / D))
    dmid_ref[...] = dmid
    low[...] = dmid.astype(BF16)
    own = pltpu.make_async_copy(low, full_ref.at[:, cols(t, COLS)], lsem)
    own.start()
    dgain_ref[...] = jnp.sum(dn * mid * inv, axis=0, keepdims=True)
    gather_tensor(1, low, full_ref, agss, agrs)
    own.wait()


def back_middle(routed, shared, mid, inv, gain, dy, cid):
    return pl.pallas_call(
        back_middle_kernel,
        out_shape=(
            jax.ShapeDtypeStruct((GROUP, COLS), F32),
            jax.ShapeDtypeStruct((1, COLS), F32),
            jax.ShapeDtypeStruct((GROUP, D), BF16),
        ),
        in_specs=[VM] * 6,
        out_specs=(VM, VM, ANY),
        scratch_shapes=[pltpu.VMEM((GROUP, COLS), BF16)]
        + sum_rows_scratch()
        + gather_sems(1)
        + [DMA],
        compiler_params=params(cid),
        name="back_middle",
    )(routed, shared, mid, inv, gain, dy)


def back_input_kernel(
    part_ref, lat_ref, x_ref, inv_ref, gain_ref, dmid_ref, ffn_ref, dx_ref, gains_ref, low, dn, *scratch
):
    rs, st, ag, lsem = scratch[:7], scratch[7:10], scratch[10:12], scratch[12]
    t = lax.axis_index("tensor")
    greet_tensor()

    def emit(r, value):
        dn[r] = value + lat_ref[r]

    scatter_tensor(1, lambda r, owner: part_ref.at[r, cols(owner, COLS)], GROUP, COLS, emit, *rs)
    xd = x_ref[...].astype(F32)
    inv = inv_ref[...]
    d = dn[...]
    u = d * gain_ref[...].astype(F32)
    row = jnp.sum(d * xd * inv, axis=0, keepdims=True)
    place = lax.broadcasted_iota(jnp.int32, (16, COLS), 0)
    both = jnp.where(place == 0, row, jnp.where(place == 1, ffn_ref[...], 0.0))
    low[...] = both.astype(BF16)
    own = pltpu.make_async_copy(low, gains_ref.at[:, cols(t, COLS)], lsem)
    own.start()
    total = sum_rows_tensor(u * xd, *st)
    dx_ref[...] = dmid_ref[...] + inv * u - xd * (inv * inv * inv * total * (1.0 / D))
    for j in range(1, TENSOR):
        to = lax.rem(t + j, TENSOR)
        dst = gains_ref.at[:, cols(t, COLS)]
        remote(low, dst, ag[0].at[j], ag[1].at[j], "tensor", to).start()
    for j in range(1, TENSOR):
        dst = gains_ref.at[:, cols(lax.rem(t + TENSOR - j, TENSOR), COLS)]
        c = remote(low, dst, ag[0].at[j], ag[1].at[j], "tensor", t)
        c.wait_recv()
        c.wait_send()
    own.wait()


def back_input(part, lat, x, inv, gain, dmid, ffn, cid):
    return pl.pallas_call(
        back_input_kernel,
        out_shape=(
            jax.ShapeDtypeStruct((GROUP, COLS), F32),
            jax.ShapeDtypeStruct((16, D), BF16),
        ),
        in_specs=[ANY] + [VM] * 6,
        out_specs=(VM, ANY),
        scratch_shapes=[pltpu.VMEM((16, COLS), BF16), pltpu.VMEM((GROUP, COLS), F32)]
        + scatter_scratch(1, GROUP, COLS, BF16)
        + sum_rows_scratch()
        + [DMA((TENSOR,)), DMA((TENSOR,)), DMA],
        compiler_params=params(cid),
        name="back_input",
    )(part, lat, x, inv, gain, dmid, ffn)


def ar_kernel(in_ref, out_ref, acc, got, ssem, rsem, ssem2, rsem2):
    t = lax.axis_index("tensor")
    greet_tensor()
    for j in range(1, TENSOR):
        to = lax.rem(t + j, TENSOR)
        remote(in_ref.at[to], got.at[t], ssem.at[j], rsem.at[j], "tensor", to).start()
    total = in_ref[t].astype(F32)
    for j in range(1, TENSOR):
        frm = lax.rem(t + TENSOR - j, TENSOR)
        c = remote(in_ref.at[t], got.at[frm], ssem.at[j], rsem.at[j], "tensor", t)
        c.wait_recv()
        c.wait_send()
        total = total + got[frm].astype(F32)
    acc[...] = total.astype(BF16)
    out_ref[t] = acc[...]
    for j in range(1, TENSOR):
        to = lax.rem(t + j, TENSOR)
        remote(acc, out_ref.at[t], ssem2.at[j], rsem2.at[j], "tensor", to).start()
    for j in range(1, TENSOR):
        frm = lax.rem(t + TENSOR - j, TENSOR)
        c = remote(acc, out_ref.at[frm], ssem2.at[j], rsem2.at[j], "tensor", t)
        c.wait_recv()
        c.wait_send()


def ar_tensor(value, cid):
    rows, n = value.shape
    part = rows // TENSOR
    out = pl.pallas_call(
        ar_kernel,
        out_shape=jax.ShapeDtypeStruct((TENSOR, part, n), value.dtype),
        in_specs=[VM],
        out_specs=VM,
        scratch_shapes=[
            pltpu.VMEM((part, n), value.dtype),
            pltpu.VMEM((TENSOR, part, n), value.dtype),
        ]
        + [DMA((TENSOR,))] * 4,
        compiler_params=params(cid),
        name="ar_tensor",
    )(value.reshape(TENSOR, part, n))
    return out.reshape(rows, n)


def a2a_expert_kernel(in_ref, out_ref, ssem, rsem, lsem):
    e = lax.axis_index("expert")
    z = e // YN
    y = lax.rem(e, YN)
    peers = []
    for dz in range(ZN):
        for dy in range(YN):
            if dz or dy:
                to = lax.rem(z + dz, ZN) * YN + lax.rem(y + dy, YN)
                frm = lax.rem(z + ZN - dz, ZN) * YN + lax.rem(y + YN - dy, YN)
                peers.append((to, frm))
    greet([("expert", to) for to, frm in peers])
    own = pltpu.make_async_copy(in_ref.at[e], out_ref.at[e], lsem)
    own.start()
    sends = []
    for j, (to, frm) in enumerate(peers):
        c = remote(in_ref.at[to], out_ref.at[e], ssem.at[j], rsem.at[j], "expert", to)
        c.start()
        sends.append(c)
    for j, (to, frm) in enumerate(peers):
        remote(out_ref.at[frm], out_ref.at[frm], ssem.at[j], rsem.at[j], "expert", to).wait_recv()
    for s in sends:
        s.wait_send()
    own.wait()


def a2a_expert(value, cid):
    n = value.shape[0]
    return pl.pallas_call(
        a2a_expert_kernel,
        out_shape=jax.ShapeDtypeStruct(value.shape, value.dtype),
        in_specs=[ANY],
        out_specs=ANY,
        scratch_shapes=[DMA((n - 1,)), DMA((n - 1,)), DMA],
        compiler_params=params(cid),
        name="a2a_expert",
    )(value)


def ag_expert_kernel(a_ref, b_ref, ao_ref, bo_ref, ssem, rsem, lsem):
    e = lax.axis_index("expert")
    z = e // YN
    y = lax.rem(e, YN)
    yr, yl, yf = lax.rem(y + 1, YN), lax.rem(y + 3, YN), lax.rem(y + 2, YN)
    zr, zl, zf = lax.rem(z + 1, ZN), lax.rem(z + 3, ZN), lax.rem(z + 2, ZN)
    y_right, y_left = z * YN + yr, z * YN + yl
    z_right, z_left = zr * YN + y, zl * YN + y
    greet([("expert", p) for p in (y_right, y_left, z_right, z_left)])
    h = a_ref.shape[0] // 2
    own_a = pltpu.make_async_copy(a_ref, ao_ref.at[z, y], lsem.at[0])
    own_b = pltpu.make_async_copy(b_ref, bo_ref.at[z, y], lsem.at[1])
    own_a.start()
    own_b.start()
    sends = []

    def send(j, src, dst, to):
        c = remote(src, dst, ssem.at[j], rsem.at[j], "expert", to)
        c.start()
        sends.append(c)

    def arrived(j, ref):
        remote(ref, ref, ssem.at[j], rsem.at[j], "expert", y_right).wait_recv()

    first, second = pl.ds(0, h), pl.ds(h, h)
    send(0, a_ref, ao_ref.at[z, y], y_right)
    send(1, a_ref, ao_ref.at[z, y], y_left)
    send(2, b_ref, bo_ref.at[z, y], z_right)
    send(3, b_ref, bo_ref.at[z, y], z_left)
    arrived(0, ao_ref.at[z, yl])
    send(4, ao_ref.at[z, yl, first], ao_ref.at[z, yl, first], y_right)
    arrived(1, ao_ref.at[z, yr])
    send(5, ao_ref.at[z, yr, second], ao_ref.at[z, yr, second], y_left)
    arrived(2, bo_ref.at[zl, y])
    send(6, bo_ref.at[zl, y, first], bo_ref.at[zl, y, first], z_right)
    arrived(3, bo_ref.at[zr, y])
    send(7, bo_ref.at[zr, y, second], bo_ref.at[zr, y, second], z_left)
    ys = (y, yl, yr, yf)
    zs = (z, zl, zr, zf)
    for i in range(4):
        if i == 3:
            arrived(4, ao_ref.at[z, yf, first])
            arrived(5, ao_ref.at[z, yf, second])
            arrived(6, bo_ref.at[zf, y, first])
            arrived(7, bo_ref.at[zf, y, second])
        sa, sb = ao_ref.at[z, ys[i]], bo_ref.at[zs[i], y]
        src_a, src_b = (a_ref, b_ref) if i == 0 else (sa, sb)
        send(8 + 4 * i, src_a, sa, z_right)
        send(9 + 4 * i, src_a, sa, z_left)
        send(10 + 4 * i, src_b, sb, y_right)
        send(11 + 4 * i, src_b, sb, y_left)
    for i in range(4):
        arrived(8 + 4 * i, ao_ref.at[zl, ys[i]])
        send(24 + 4 * i, ao_ref.at[zl, ys[i], first], ao_ref.at[zl, ys[i], first], z_right)
        arrived(9 + 4 * i, ao_ref.at[zr, ys[i]])
        send(25 + 4 * i, ao_ref.at[zr, ys[i], second], ao_ref.at[zr, ys[i], second], z_left)
        arrived(10 + 4 * i, bo_ref.at[zs[i], yl])
        send(26 + 4 * i, bo_ref.at[zs[i], yl, first], bo_ref.at[zs[i], yl, first], y_right)
        arrived(11 + 4 * i, bo_ref.at[zs[i], yr])
        send(27 + 4 * i, bo_ref.at[zs[i], yr, second], bo_ref.at[zs[i], yr, second], y_left)
    for i in range(4):
        arrived(24 + 4 * i, ao_ref.at[zf, ys[i], first])
        arrived(25 + 4 * i, ao_ref.at[zf, ys[i], second])
        arrived(26 + 4 * i, bo_ref.at[zs[i], yf, first])
        arrived(27 + 4 * i, bo_ref.at[zs[i], yf, second])
    for s in sends:
        s.wait_send()
    own_a.wait()
    own_b.wait()


def ag_expert(a, b, cid):
    shape = jax.ShapeDtypeStruct((ZN, YN) + a.shape, a.dtype)
    ao, bo = pl.pallas_call(
        ag_expert_kernel,
        out_shape=(shape, shape),
        in_specs=[ANY, ANY],
        out_specs=(ANY, ANY),
        scratch_shapes=[DMA((40,)), DMA((40,)), DMA((2,))],
        compiler_params=params(cid),
        name="ag_expert",
    )(a, b)
    return ao.reshape((GROUPS,) + a.shape), bo.reshape((GROUPS,) + a.shape)


def dot_nn(a, b):
    return lax.dot_general(a, b, (((1,), (0,)), ((), ())), preferred_element_type=F32)


def dot_nt(a, b):
    return lax.dot_general(a, b, (((1,), (1,)), ((), ())), preferred_element_type=F32)


def dot_tn(a, b):
    return lax.dot_general(a, b, (((0,), (0,)), ((), ())), preferred_element_type=F32)


def expert_kernel(rows_ref, grad_ref, wg_ref, wu_ref, wd_ref, part_ref, drows_ref, gg_ref, gu_ref, gd_ref):
    n = GROUPS * PADCAP
    rows = rows_ref[...].reshape(n, D)
    grad = grad_ref[...].reshape(n, D)
    wg, wu, wd = wg_ref[0], wu_ref[0], wd_ref[0]
    gate = dot_nt(rows, wg)
    up = dot_nt(rows, wu)
    sig = jax.nn.sigmoid(gate)
    silu = gate * sig
    hidden = (silu * up).astype(BF16)
    part_ref[...] = dot_nn(hidden, wd).astype(BF16).reshape(part_ref.shape)
    gd_ref[0] = dot_tn(hidden, grad)
    dh = dot_nt(grad, wd)
    dg = (dh * up * (sig * (1.0 + gate * (1.0 - sig)))).astype(BF16)
    du = (dh * silu).astype(BF16)
    gg_ref[0] = dot_tn(dg, rows)
    gu_ref[0] = dot_tn(du, rows)
    drows_ref[...] = (dot_nn(dg, wg) + dot_nn(du, wu)).astype(BF16).reshape(drows_ref.shape)


def expert_step(rows, grads, wg, wu, wd):
    hid = wd.shape[1]
    block = pl.BlockSpec((GROUPS, 1, PADCAP, D), lambda i: (0, i, 0, 0))
    weight = pl.BlockSpec((1, hid, D), lambda i: (i, 0, 0))
    shape = jax.ShapeDtypeStruct((GROUPS, LOCAL, PADCAP, D), BF16)
    wshape = jax.ShapeDtypeStruct((LOCAL, hid, D), F32)
    return pl.pallas_call(
        expert_kernel,
        grid=(LOCAL,),
        out_shape=(shape, shape, wshape, wshape, wshape),
        in_specs=[block, block, weight, weight, weight],
        out_specs=(block, block, weight, weight, weight),
        compiler_params=pltpu.CompilerParams(vmem_limit_bytes=60 * MIB),
        cost_estimate=pl.CostEstimate(
            flops=9 * 2 * 2048 * 2048 * hid, bytes_accessed=60 * MIB, transcendentals=0
        ),
        name="expert_step",
    )(
        rows.reshape(GROUPS, LOCAL, PADCAP, D),
        grads.reshape(GROUPS, LOCAL, PADCAP, D),
        wg,
        wu,
        wd,
    )


def rms_scale(value, gain):
    return value * lax.rsqrt(jnp.mean(value * value, axis=-1, keepdims=True) + EPS) * gain


def rotate(value, cosine, sine):
    half = value.shape[-1] // 2
    first = value[..., :half]
    second = value[..., half:]
    return jnp.concatenate(
        [first * cosine - second * sine, second * cosine + first * sine], axis=-1
    )


def pick(index, table):
    numbers = jnp.arange(table.shape[0], dtype=jnp.int32)
    return jnp.sum(jnp.where(index[:, None] == numbers[None, :], table[None, :], 0), axis=1)


def exclusive(values):
    numbers = jnp.arange(values.shape[0], dtype=jnp.int32)
    return jnp.sum(jnp.where(numbers[:, None] > numbers[None, :], values[None, :], 0), axis=1)


def deal_rows(lengths, order, group):
    begins = exclusive(lengths)
    dealt_begins = exclusive(pick(order, lengths))
    dealt_source = pick(order, begins)
    numbers = jnp.arange(lengths.shape[0], dtype=jnp.int32)
    inverse = jnp.sum(jnp.where(order[None, :] == numbers[:, None], numbers[None, :], 0), axis=1)
    given_target = pick(inverse, dealt_begins)
    rows = group * GROUP + jnp.arange(GROUP, dtype=jnp.int32)
    which = jnp.sum((rows[:, None] >= dealt_begins[None, :]).astype(jnp.int32), axis=1) - 1
    offsets = rows - pick(which, dealt_begins)
    source = pick(which, dealt_source) + offsets
    owner = jnp.sum((rows[:, None] >= begins[None, :]).astype(jnp.int32), axis=1) - 1
    target = pick(owner, given_target - begins) + rows
    return source, target, offsets, which


def one_hot_rows(index, count):
    numbers = jnp.arange(count, dtype=jnp.int32)
    return (index[:, None] == numbers[None, :]).astype(BF16)


def per_device(
    tokens,
    cotangent,
    attn_gain,
    w_query,
    w_latent,
    latent_gain,
    w_expand,
    w_out,
    ffn_gain,
    shared_gate,
    shared_up,
    shared_down,
    expert_gate,
    expert_up,
    expert_down,
    seq_lengths,
    seq_order,
    routes,
    gate_weights,
):
    group = lax.axis_index("expert")
    column = lax.axis_index("tensor")
    total = GROUP * GROUPS
    source, target, offsets, which = deal_rows(seq_lengths, seq_order, group)

    all_x, all_dy = ag_expert(tokens, cotangent, 0)
    take = one_hot_rows(source, total)
    x_cols = dot_nn(take, all_x.reshape(total, COLS)).astype(BF16)
    dy_cols = dot_nn(take, all_dy.reshape(total, COLS)).astype(BF16)
    x_full = ag_tensor(x_cols, 1)
    dy_full = lax.all_gather(dy_cols, "tensor", axis=1, tiled=True)

    chosen = routes.T
    gates = gate_weights.T
    experts = jnp.arange(EXPERTS, dtype=jnp.int32)
    hit = chosen[:, None, :] == experts[None, :, None]
    member = jnp.sum(hit.astype(F32), axis=0)
    gate_of = jnp.sum(jnp.where(hit, gates[:, None, :], 0.0), axis=0)
    token = jnp.arange(GROUP, dtype=jnp.int32)
    earlier = (token[:, None] < token[None, :]).astype(BF16)
    count = dot_nn(member.astype(BF16), earlier)
    slot = jnp.where((member > 0.5) & (count < CAP - 0.5), count, -1.0).astype(jnp.int32)
    seats = jnp.arange(PADCAP, dtype=jnp.int32)
    match = slot[:, None, :] == seats[None, :, None]
    place = match.astype(BF16).reshape(EXPERTS * PADCAP, GROUP)
    weight = jnp.where(match, gate_of[:, None, :], 0.0)
    slot_gate = jnp.sum(weight, axis=2).reshape(EXPERTS * PADCAP, 1)
    weight = weight.reshape(EXPERTS * PADCAP, GROUP)
    weight_high = lax.reduce_precision(weight, 8, 7)
    weight_low = (weight - weight_high).astype(BF16)
    weight_high = weight_high.astype(BF16)

    slot_grad = (slot_gate * dot_nn(place, dy_cols)).astype(BF16)
    slot_grad = slot_grad.reshape(GROUPS, LOCAL * PADCAP, COLS)
    slot_grad = lax.all_to_all(slot_grad, "expert", split_axis=0, concat_axis=0, tiled=True)
    grad_rows = lax.all_gather(slot_grad.reshape(-1, COLS), "tensor", axis=1, tiled=True)

    attn_gainf = attn_gain.astype(F32)
    latent_gainf = latent_gain.astype(F32)
    half = ROPE // 2
    freqs = jnp.exp(-jnp.log(10000.0) * jnp.arange(half, dtype=F32) / half)
    angles = offsets.astype(F32)[:, None] * freqs[None, :]
    cosine, sine = jnp.cos(angles), jnp.sin(angles)
    dealt = x_full.astype(F32)
    inv_one = lax.rsqrt(jnp.mean(dealt * dealt, axis=-1, keepdims=True) + EPS)
    normed = (dealt * inv_one * attn_gainf).astype(BF16)
    heads = w_query.shape[1] // HEAD
    scale = HEAD ** (-0.5)
    query_pre = dot_nn(normed, w_query).reshape(GROUP, heads, HEAD)
    cos_h, sin_h = cosine[:, None, :], sine[:, None, :]
    query = jnp.concatenate(
        [query_pre[..., :NOPE], rotate(query_pre[..., NOPE:], cos_h, sin_h)], axis=-1
    ).astype(BF16)
    latent = dot_nn(normed, w_latent)
    key_rope = rotate(latent[:, LATENT:], cosine, sine).astype(BF16)
    latent_main = latent[:, :LATENT]
    compressed = rms_scale(latent_main, latent_gainf).astype(BF16)
    expanded = dot_nn(compressed, w_expand).astype(BF16).reshape(GROUP, heads, NOPE + VDIM)
    keys = jnp.concatenate(
        [expanded[..., :NOPE], jnp.broadcast_to(key_rope[:, None, :], (GROUP, heads, ROPE))],
        axis=-1,
    )
    values = expanded[..., NOPE:]
    allowed = (which[:, None] == which[None, :]) & (token[:, None] >= token[None, :])
    raw = jnp.einsum("qhd,khd->hqk", query, keys, preferred_element_type=F32) * scale
    scores = jnp.where(allowed[None], raw, -1e30)
    peak = jnp.max(scores, axis=-1, keepdims=True)
    expo = jnp.exp(scores - peak)
    probs = expo / jnp.sum(expo, axis=-1, keepdims=True)
    probs_low = probs.astype(BF16)
    mixed = jnp.einsum("hqk,khd->qhd", probs_low, values, preferred_element_type=F32)
    mixed = mixed.astype(BF16).reshape(GROUP, heads * VDIM)
    attn_part = dot_nn(mixed, w_out)

    def own_cols(vector):
        return lax.dynamic_slice_in_dim(vector, column * COLS, COLS, 0).reshape(1, COLS)

    middle, inv_two, normed_two_cols, normed_two = middle_step(
        attn_part, x_cols, own_cols(ffn_gain), 2
    )

    outgoing = dot_nn(place, normed_two_cols).astype(BF16)
    received = a2a_expert(outgoing.reshape(GROUPS, LOCAL * PADCAP, COLS), 3)
    rows = ag_tensor(received.reshape(-1, COLS), 4, 4)

    sg_t, su_t = shared_gate.T, shared_up.T
    shared_g = dot_nt(normed_two, sg_t)
    shared_u = dot_nt(normed_two, su_t)
    shared_sig = jax.nn.sigmoid(shared_g)
    shared_silu = shared_g * shared_sig
    shared_h = (shared_silu * shared_u).astype(BF16)
    shared_part = dot_nn(shared_h, shared_down).astype(BF16)
    grad_sh = dot_nt(dy_full, shared_down)
    grad_sg = (
        grad_sh * shared_u * (shared_sig * (1.0 + shared_g * (1.0 - shared_sig)))
    ).astype(BF16)
    grad_su = (grad_sh * shared_silu).astype(BF16)
    shared_grad = (dot_nn(grad_sg, sg_t) + dot_nn(grad_su, su_t)).astype(BF16)
    shared_sum = rs_tensor(jnp.concatenate([shared_part, shared_grad], axis=0), 5, 1, F32)
    shared_weights = jnp.concatenate(
        [
            dot_tn(normed_two, grad_sg).astype(BF16),
            dot_tn(normed_two, grad_su).astype(BF16),
            dot_tn(dy_full, shared_h).astype(BF16),
        ],
        axis=1,
    )
    shared_weights = lax.psum_scatter(
        shared_weights, "expert", scatter_dimension=0, tiled=True
    ).astype(F32)
    wide = shared_g.shape[1]
    grad_sgate = shared_weights[:, :wide]
    grad_sup = shared_weights[:, wide : 2 * wide]
    grad_sdown = shared_weights[:, 2 * wide :].T

    part, drows, grad_eg, grad_eu, grad_ed = expert_step(
        rows,
        grad_rows,
        jnp.swapaxes(expert_gate, 1, 2),
        jnp.swapaxes(expert_up, 1, 2),
        expert_down,
    )
    back = rs_tensor(drows.reshape(-1, D), 6, 4)
    back = a2a_expert(back.reshape(GROUPS, LOCAL * PADCAP, COLS), 7)
    routed_grad = dot_tn(place, back.reshape(-1, COLS))

    returned = lax.psum_scatter(part.reshape(-1, D), "tensor", scatter_dimension=1, tiled=True)
    returned = lax.all_to_all(
        returned.reshape(GROUPS, LOCAL * PADCAP, COLS),
        "expert",
        split_axis=0,
        concat_axis=0,
        tiled=True,
    ).reshape(-1, COLS)
    routed = dot_tn(weight_high, returned) + dot_tn(weight_low, returned)
    output_cols = (middle + shared_sum[:GROUP] + routed).astype(BF16)
    all_out = lax.all_gather(output_cols, "expert", axis=0, tiled=True)

    dmid, dgain_ffn, d_attn = back_middle(
        routed_grad, shared_sum[GROUP:], middle, inv_two, own_cols(ffn_gain), dy_cols, 8
    )

    grad_wout = dot_tn(d_attn, mixed).astype(BF16)
    grad_mixed = dot_nt(d_attn, w_out).astype(BF16).reshape(GROUP, heads, VDIM)
    grad_values = jnp.einsum("hqk,qhd->khd", probs_low, grad_mixed, preferred_element_type=F32)
    grad_probs = jnp.einsum("qhd,khd->hqk", grad_mixed, values, preferred_element_type=F32)
    grad_scores = (
        probs * (grad_probs - jnp.sum(grad_probs * probs, axis=-1, keepdims=True))
    ).astype(BF16)
    grad_query = jnp.einsum("hqk,khd->qhd", grad_scores, keys, preferred_element_type=F32) * scale
    grad_keys = jnp.einsum("hqk,qhd->khd", grad_scores, query, preferred_element_type=F32) * scale
    grad_qpre = jnp.concatenate(
        [grad_query[..., :NOPE], rotate(grad_query[..., NOPE:], cos_h, -sin_h)], axis=-1
    )
    grad_qpre = grad_qpre.astype(BF16).reshape(GROUP, heads * HEAD)
    rope_part = jnp.sum(grad_keys[..., NOPE:], axis=1)
    grad_expanded = jnp.concatenate([grad_keys[..., :NOPE], grad_values], axis=-1)
    grad_expanded = grad_expanded.astype(BF16).reshape(GROUP, heads * (NOPE + VDIM))
    grad_wexp = dot_tn(compressed, grad_expanded).astype(BF16)
    compressed_part = dot_nt(grad_expanded, w_expand)
    summed = ar_tensor(
        jnp.concatenate(
            [compressed_part, rope_part, jnp.zeros((GROUP, ROPE), F32)], axis=1
        ).astype(BF16),
        9,
    ).astype(F32)
    grad_wq = dot_tn(normed, grad_qpre).astype(BF16)
    normed_part = dot_nt(grad_qpre, w_query).astype(BF16)
    unused, latent_norm_back = jax.vjp(rms_scale, latent_main, latent_gainf)
    grad_lmain, grad_lgain = latent_norm_back(summed[:, :LATENT])
    grad_lrope = rotate(summed[:, LATENT : LATENT + ROPE], cosine, -sine)
    grad_latent_low = jnp.concatenate([grad_lmain, grad_lrope], axis=-1).astype(BF16)
    grad_wlat = dot_tn(normed, grad_latent_low).astype(BF16)
    own_latent = lax.dynamic_slice_in_dim(w_latent, column * COLS, COLS, 0)
    latent_cols = dot_nt(grad_latent_low, own_latent)
    dx_cols, gains = back_input(
        normed_part, latent_cols, x_cols, inv_one, own_cols(attn_gain), dmid, dgain_ffn, 10
    )

    def sum_groups(value):
        moved = lax.all_to_all(value, "expert", split_axis=0, concat_axis=0, tiled=True)
        return jnp.sum(
            moved.reshape(GROUPS, moved.shape[0] // GROUPS, moved.shape[1]).astype(F32), axis=0
        )

    grad_wq = sum_groups(grad_wq)
    grad_wlat = sum_groups(grad_wlat)
    grad_wexp = sum_groups(grad_wexp)
    grad_wout = sum_groups(grad_wout).T

    extra = jnp.concatenate(
        [gains[:2].reshape(16, COLS), grad_lgain.astype(BF16).reshape(2, COLS)], axis=0
    )
    bundle = jnp.concatenate(
        [dx_cols.astype(BF16), extra, jnp.zeros((14, COLS), BF16)], axis=0
    )
    left, right = ag_expert(bundle[:, : COLS // 2], bundle[:, COLS // 2 :], 11)
    back_take = one_hot_rows(target, total)
    output = dot_nn(back_take, all_out).astype(BF16)
    input_grad = jnp.concatenate(
        [
            dot_nn(back_take, side[:, :GROUP].reshape(total, COLS // 2)).astype(BF16)
            for side in (left, right)
        ],
        axis=1,
    )
    sums = jnp.concatenate(
        [
            jnp.sum(side[:, GROUP : GROUP + 18].astype(F32), axis=0)
            for side in (left, right)
        ],
        axis=1,
    )
    gain_grads = sums[:16].reshape(2, D)
    lgain_grad = sums[16:].reshape(LATENT)
    own = lax.dynamic_slice_in_dim(gain_grads, group * (D // GROUPS), D // GROUPS, 1)
    own_l = lax.dynamic_slice_in_dim(lgain_grad, group * (LATENT // GROUPS), LATENT // GROUPS, 0)
    return (
        output,
        input_grad,
        own[0],
        grad_wq,
        grad_wlat,
        own_l,
        grad_wexp,
        grad_wout,
        own[1],
        grad_sgate,
        grad_sup,
        grad_sdown,
        jnp.swapaxes(grad_eg, 1, 2),
        jnp.swapaxes(grad_eu, 1, 2),
        grad_ed,
    )


def solution(mesh):
    return jax.shard_map(
        per_device,
        mesh=mesh,
        in_specs=(
            P("expert", "tensor"),
            P("expert", "tensor"),
            P(),
            P(None, "tensor"),
            P(),
            P(),
            P(None, "tensor"),
            P("tensor", None),
            P(),
            P(None, "tensor"),
            P(None, "tensor"),
            P("tensor", None),
            P("expert", None, "tensor"),
            P("expert", None, "tensor"),
            P("expert", "tensor", None),
            P(),
            P(),
            P("expert", None),
            P("expert", None),
        ),
        out_specs=(
            P("expert", "tensor"),
            P("expert", "tensor"),
            P("expert"),
            P("expert", "tensor"),
            P("expert", None),
            P("expert"),
            P("expert", "tensor"),
            P("tensor", "expert"),
            P("expert"),
            P("expert", "tensor"),
            P("expert", "tensor"),
            P("tensor", "expert"),
            P("expert", None, "tensor"),
            P("expert", None, "tensor"),
            P("expert", "tensor", None),
        ),
        check_vma=False,
    )
```

time: 1640 us -> 607 us (0.37)
  waiting for transfers between devices: 705 us -> 11.7 us
  Pallas kernels: 0 us -> 366 us
  other arithmetic: 381 us -> 44.5 us
  local copies, waits for them, and re-layouts: 282 us -> 58.3 us
  matrix products: 135 us -> 54.1 us
  blocking collectives: 73.3 us -> 19.9 us
    pallas_call x0 -> x13, Pallas kernels: none -> 366 us  [the longest x2 77.1 us: ag_expert(): pl.pallas_call(ag_expert_kernel, out_shape=(shape, shape), in_specs=[ANY,...]
    unnamed x21 -> x6, waiting for transfers between devices: 294 us -> 0.09 us
    gather x19 -> x0, other arithmetic: 208 us -> none  [the longest x8 124 us: deal_layout(): target = dispatched_starts[inverse_seq[owner]] + places - begins[owner]]
    all_to_all x4 -> x5, waiting for transfers between devices: 179 us -> 11.6 us  [the longest x4 7.17 us: sum_groups(): lax.all_to_all(value, 'expert', split_axis=0, concat_axis=0, tiled=True)]
    gather x26 -> x0, local copies, waits for them, and re-layouts: 115 us -> none  [the longest x2 28.8 us: per_device(): grad_dealt[slot_token]]
    reduce_scatter x3 -> x1, waiting for transfers between devices: 92.4 us -> 0.01 us  [per_device(): lax.psum_scatter(part.reshape(-1, D), 'tensor', scatter_dimension=1, tile...]
    psum x3 -> x0, waiting for transfers between devices: 87.5 us -> none  [the longest x1 67.2 us: per_device(): attn = lax.psum(product(mixed, w_out), 'tensor')]
    dot_general x35 -> x36, matrix products: 135 us -> 49.5 us  [the longest x15 20.8 us: dot_nn(): lax.dot_general(a, b, (((1,), (0,)), ((), ())), preferred_element_type=F32)]
  transfers between devices with their start and end apart: 20 -> 10, of which waited for: 13 -> 2; matrix products, arithmetic and copies ran while one was open for 44% -> 23% of each run, Pallas kernels for 0% -> 56%
where the time goes in v1:
time: 607 us; the launch traced here: 599 us
  Pallas kernels  366 us (60%)
  local copies, waits for them, and re-layouts  58.3 us (10%)
  matrix products  54.1 us (9%)
  other arithmetic  44.5 us (7%)
  starting transfers between devices  29.1 us (5%)
  blocking collectives  19.9 us (3%)
  between operations  15.3 us (3%)
  waiting for transfers between devices  11.7 us (2%)
    pallas_call x2, Pallas kernels, ag_expert(): pl.pallas_call(ag_expert_kernel, out_shape=(shape, shape), in_specs=[ANY,...  77.1 us
    pallas_call x2, Pallas kernels, rs_tensor(): pl.pallas_call(functools.partial(rs_tensor_kernel, nch), out_shape=jax.Sh...  70.8 us
    pallas_call x2, Pallas kernels, ag_tensor(): pl.pallas_call(functools.partial(ag_tensor_kernel, nch), out_shape=jax.Sh...  55 us
    pallas_call x2, Pallas kernels, a2a_expert(): pl.pallas_call(a2a_expert_kernel, out_shape=jax.ShapeDtypeStruct(value.sh...  40 us
    pallas_call x1, Pallas kernels, middle_step(): pl.pallas_call(middle_kernel, out_shape=(jax.ShapeDtypeStruct((GROUP, COL...  39 us
    unnamed x166, local copies, waits for them, and re-layouts  30 us
    pallas_call x1, Pallas kernels, expert_step(): pl.pallas_call(expert_kernel, grid=(LOCAL,), out_shape=(shape, shape, wsh...  29.6 us
    pallas_call x1, Pallas kernels, back_input(): pl.pallas_call(back_input_kernel, out_shape=(jax.ShapeDtypeStruct((GROUP,...  22 us
  transfers between devices with their start and end apart: 10, of which 2 were waited for; matrix products, arithmetic and copies ran while one was open for 23% of the time, Pallas kernels for 56%

profile of v1, /device:TPU:1, one launch (start us, length us, event | category | flops | bytes accessed | tf_op | source)
XLA Modules:
  0.0 598.8 jit_solution(10753482395329310620)
XLA Ops:
  11.5 29.5 %ag_expert.2 = (bf16[4,4,256,256]{3,2,1,0:T(8,128)(2,1)S(1)}, bf16[4,4,256,256]{3,2,1,0:T(8,128)(2,1)S(1)}) custom-call(bf16[256,256]{1,0:T(8,128)(2,1)S(1)} %copy-done.20, bf16[256,256]{1,0:T(8,128)(2,1)S(1)} %copy-done.21), custom_call_target="tpu_custom_call" | custom-call | tf_op jit(solution)/shard_map/ag_expert/pallas_call | solution.py:580
  46.0 1.7 fusion.12
  48.3 19.9 %all_to_all.46 = bf16[16,128,256]{2,1,0:T(8,128)(2,1)} all-to-all(bf16[16,128,256]{2,1,0:T(8,128)(2,1)S(1)} %bitcast.139), channel_id=1, replica_groups=mesh['expert'=16,'tensor'=8] {'expert'}, dimensions={0} | all-to-all | bytes 2097152 | tf_op jit(solution)/shard_map/all_to_all | solution.py:749
  68.8 2.4 fusion.27.in_ref.x_ref
  71.2 14.4 %ag_tensor.2 = bf16[256,2048]{1,0:T(8,128)(2,1)S(1)} custom-call(bf16[256,256]{1,0:T(8,128)(2,1)S(1)} %fusion.27.in_ref.x_ref), custom_call_target="tpu_custom_call" | custom-call | tf_op jit(solution)/shard_map/ag_tensor/pallas_call | solution.py:252
  88.9 1.8 copy.110
  90.7 1.6 slice.147
  92.2 2.2 fusion.79
  99.2 1.5 subtract_convert_fusion.1
  101.3 2.2 fusion.86
  103.6 2.3 convolution_convert_fusion.12
  105.9 1.9 fusion.87.part_ref
  107.8 39.0 %middle_step.1 = (f32[256,256]{1,0:T(8,128)S(1)}, f32[256,1]{1,0:T(8,128)S(1)}, bf16[256,256]{1,0:T(8,128)(2,1)S(1)}, bf16[256,2048]{1,0:T(8,128)(2,1)S(1)}) custom-call(f32[256,2048]{1,0:T(8,128)S(1)} %fusion.87.part_ref, bf16[256,256]{1,0:T(8,128)(2,1)S(1)} %fusion.27.in_ref.x_ref, bf16[1,256]{1,0:T(2,128)(2,1)S(1)} %reshape.474.gain_ref), custom_call_target="tpu_custom_call" | custom-call | tf_op jit(solution)/shard_map/middle_step/pallas_call | solution.py:312
  151.0 2.4 fusion.89
  156.1 2.3 pad_maximum_fusion
  158.4 6.5 %copy.108 = bf16[2048,1056]{1,0:T(8,128)(2,1)} copy(bf16[2048,1056]{0,1:T(8,128)(2,1)} %pad_maximum_fusion) | data formatting | bytes 8650752
  166.5 20.2 %a2a_expert.2 = bf16[16,128,256]{2,1,0:T(8,128)(2,1)S(1)} custom-call(bf16[16,128,256]{2,1,0:T(8,128)(2,1)S(1)} %bitcast.123), custom_call_target="tpu_custom_call" | custom-call | tf_op jit(solution)/shard_map/a2a_expert/pallas_call | solution.py:496
  186.7 40.5 %ag_tensor.3 = bf16[2048,2048]{1,0:T(8,128)(2,1)} custom-call(bf16[2048,256]{1,0:T(8,128)(2,1)S(1)} %bitcast.121), custom_call_target="tpu_custom_call" | custom-call | tf_op jit(solution)/shard_map/ag_tensor/pallas_call | solution.py:252
  227.3 29.6 %expert_step.1 = (bf16[16,4,32,2048]{3,2,1,0:T(8,128)(2,1)}, bf16[16,4,32,2048]{3,2,1,0:T(8,128)(2,1)}, f32[4,176,2048]{2,1,0:T(8,128)}, f32[4,176,2048]{2,1,0:T(8,128)}, f32[4,176,2048]{2,1,0:T(8,128)}) custom-call(bf16[16,4,32,2048]{3,2,1,0:T(8,128)(2,1)} %bitcast.133, bf16[16,4,32,2048]{3,2,1,0:T(8,128)(2,1)} %bitcast.164, ...), custom_call_target="tpu_custom_call" | custom-call | flops 13287555072 | bytes 62914560 | tf_op jit(solution)/shard_map/expert_step/pallas_call | solution.py:630
  263.8 2.0 iota_compare_fusion.7
  265.8 2.2 convolution_convert_fusion.8
  270.3 19.8 %rs_tensor.2 = f32[512,256]{1,0:T(8,128)S(1)} custom-call(bf16[512,2048]{1,0:T(8,128)(2,1)S(1)} %pad_maximum_fusion.1.in_ref), custom_call_target="tpu_custom_call" | custom-call | tf_op jit(solution)/shard_map/rs_tensor/pallas_call | solution.py:279
  291.8 1.8 copy.109
  293.6 1.8 convert_element_type.265
  295.4 1.7 fusion.84
  297.1 51.0 %rs_tensor.3 = bf16[2048,256]{1,0:T(8,128)(2,1)S(1)} custom-call(bf16[2048,2048]{1,0:T(8,128)(2,1)} %bitcast.132), custom_call_target="tpu_custom_call" | custom-call | tf_op jit(solution)/shard_map/rs_tensor/pallas_call | solution.py:279
  348.1 19.8 %a2a_expert.3 = bf16[16,128,256]{2,1,0:T(8,128)(2,1)S(1)} custom-call(bf16[16,128,256]{2,1,0:T(8,128)(2,1)S(1)} %bitcast.122), custom_call_target="tpu_custom_call" | custom-call | tf_op jit(solution)/shard_map/a2a_expert/pallas_call | solution.py:496
  368.8 17.8 %back_middle.1 = (f32[256,256]{1,0:T(8,128)S(1)}, f32[1,256]{1,0:T(1,128)S(1)}, bf16[256,2048]{1,0:T(8,128)(2,1)S(1)}) custom-call(f32[256,256]{1,0:T(8,128)S(1)} %fusion.92.routed_ref, f32[256,256]{1,0:T(8,128)S(1)} %copy-done.13, f32[256,256]{1,0:T(8,128)S(1)} %copy-done.11, f32[256,1]{1,0:T(8,128)S(1)} %copy-done.19, ...), custom_call_target="tpu_custom_call" | custom-call | tf_op jit(solution)/shard_map/back_middle/pallas_call | solution.py:353
  390.1 2.4 convolution_bitcast_fusion
  392.5 1.7 maximum_convert_fusion
  394.2 1.8 copy.92
  396.0 1.8 convert_element_type.243
  397.8 2.3 convolution_convert_fusion.9
  400.1 4.7 all-to-all-start.4
  404.7 2.2 convolution_convert_fusion.10
  406.9 1.5 slice_reduce_fusion
  411.0 14.5 %ar_tensor.1 = bf16[8,32,640]{2,1,0:T(8,128)(2,1)S(1)} custom-call(bf16[8,32,640]{2,1,0:T(8,128)(2,1)S(1)} %maximum_maximum_fusion.in_ref), custom_call_target="tpu_custom_call" | custom-call | tf_op jit(solution)/shard_map/ar_tensor/pallas_call | solution.py:452
  426.4 6.9 %all-to-all-start.1 = ((bf16[16,128,256]{2,1,0:T(8,128)(2,1)}), bf16[16,128,256]{2,1,0:T(8,128)(2,1)}, u32[]{:S(2)}, u32[]{:S(2)}) async-start(bf16[16,128,256]{2,1,0:T(8,128)(2,1)} %bitcast.143), calls=%async_computation.2 | async-start | bytes 2097152 | tf_op jit(solution)/shard_map/all_to_all | solution.py:842
  433.3 1.7 fusion.83
  435.1 1.6 copy.112
  436.7 1.6 copy.113
  440.3 1.6 fusion.55
  443.3 2.4 convolution_convert_fusion.6
  445.7 4.4 all-to-all-done.1
  450.1 4.4 all-to-all-start.5
  455.7 2.8 convolution_convert_fusion.1
  458.5 1.7 fusion.91
  460.3 2.4 fusion.25
  462.7 7.2 %all-to-all-done.5 = bf16[16,128,256]{2,1,0:T(8,128)(2,1)} async-done(((bf16[16,128,256]{2,1,0:T(8,128)(2,1)}), bf16[16,128,256]{2,1,0:T(8,128)(2,1)}, u32[]{:S(2)}, u32[]{:S(2)}) %all-to-all-start.5) | async-done | bytes 1048608 | tf_op jit(solution)/shard_map/all_to_all | solution.py:895
  469.9 5.0 all-to-all-start.2
  474.9 1.6 slice_bitcast_fusion
  476.5 1.9 slice.155
  478.4 2.0 copy.111
  480.4 2.0 multiply_reduce_fusion.1
  488.4 22.0 %back_input.1 = (f32[256,256]{1,0:T(8,128)S(1)}, bf16[16,2048]{1,0:T(8,128)(2,1)S(1)}) custom-call(bf16[256,2048]{1,0:T(8,128)(2,1)S(1)} %convolution_convert_fusion.5.part_ref, f32[256,256]{1,0:T(8,128)S(1)} %fusion.34.lat_ref, bf16[256,256]{1,0:T(8,128)(2,1)S(1)} %fusion.27.in_ref.x_ref, f32[256,1]{1,0:T(8,128)S(1)} %copy-done.14, ...), custom_call_target="tpu_custom_call" | custom-call | tf_op jit(solution)/shard_map/back_input/pallas_call | solution.py:407
  512.2 1.9 fusion.18
  514.1 2.0 copy.117
  516.1 7.3 %all-to-all-start.3 = ((bf16[16,128,576]{1,2,0:T(8,128)(2,1)}), bf16[16,128,576]{1,2,0:T(8,128)(2,1)}, u32[]{:S(2)}, u32[]{:S(2)}) async-start(bf16[16,128,576]{1,2,0:T(8,128)(2,1)} %bitcast.131), calls=%async_computation.4 | async-start | bytes 4718592 | tf_op jit(solution)/shard_map/all_to_all | solution.py:895
  523.5 47.6 %ag_expert.3 = (bf16[4,4,288,128]{3,2,1,0:T(8,128)(2,1)S(1)}, bf16[4,4,288,128]{3,2,1,0:T(8,128)(2,1)S(1)}) custom-call(bf16[288,128]{1,0:T(8,128)(2,1)S(1)} %get-tuple-element.136.a_ref, bf16[288,128]{1,0:T(8,128)(2,1)S(1)} %get-tuple-element.135.b_ref), custom_call_target="tpu_custom_call" | custom-call | tf_op jit(solution)/shard_map/ag_expert/pallas_call | solution.py:580
  575.0 1.7 copy.99
  580.0 1.8 convert_reduce_fusion.3
  583.9 2.3 convert_reduce_fusion.1
  586.2 2.7 convert_reduce_fusion
  588.9 3.0 fusion.26
  (268 shorter events, 67.2 us)
Async XLA Ops:
  7.2 78.8 %copy-start = (bf16[2048,576]{0,1:T(8,128)(2,1)S(1)}, bf16[2048,576]{0,1:T(8,128)(2,1)}, u32[]{:S(2)}) copy-start(bf16[2048,576]{0,1:T(8,128)(2,1)} %param.23) | copy-start | bytes 7077892
  7.2 143.8 %all-gather.4.cloned.1.call-start = ((), (), s32[]{:S(2)}) async-start(), calls=%async_computation.8 | async-start | bytes 1179648 | tf_op jit(solution)/shard_map/all_gather | solution.py:725
  8.2 37.0 %copy-start.74 = (s32[64]{0:T(128)}, s32[64]{0:T(128)S(1)}, u32[]{:S(2)}) copy-start(s32[64]{0:T(128)S(1)} %select_reduce_fusion.10) | copy-start | bytes 772
  11.5 33.6 %copy-start.76 = (s32[64]{0:T(128)}, s32[64]{0:T(128)S(1)}, u32[]{:S(2)}) copy-start(s32[64]{0:T(128)S(1)} %select_reduce_fusion.7) | copy-start | bytes 772
  43.1 2.2 copy-start.66
  43.1 2.2 copy-start.67
  45.1 2.7 copy-start.7
  45.2 182.1 %all-gather.6.cloned.1.call-start = ((), (), s32[]{:S(2)}) async-start(), calls=%async_computation.9 | async-start | bytes 9437184 | tf_op jit(solution)/shard_map/all_gather | solution.py:750
  45.5 2.8 copy-start.45
  46.0 22.2 %copy-start.27 = (pred[2048,256]{1,0:T(32,128)(4,1)}, pred[2048,256]{1,0:T(32,128)(4,1)S(1)}, u32[]{:S(2)}) copy-start(pred[2048,256]{1,0:T(32,128)(4,1)S(1)} %bitcast_compare_fusion) | copy-start | bytes 1572868
  68.2 223.5 %reduce-scatter.7.cloned.1.call-start = ((), (), s32[]{:S(2)}) async-start(), calls=%async_computation.12 | async-start | bytes 5013504
  68.8 16.8 %copy-start.70 = (bf16[2048]{0:T(1024)(128)(2,1)S(1)}, bf16[2048]{0:T(1024)(128)(2,1)}, u32[]{:S(2)}) copy-start(bf16[2048]{0:T(1024)(128)(2,1)} %param.21) | copy-start | bytes 12292
  68.8 16.8 %copy-start.77 = (bf16[512]{0:T(512)(128)(2,1)S(1)}, bf16[512]{0:T(512)(128)(2,1)}, u32[]{:S(2)}) copy-start(bf16[512]{0:T(512)(128)(2,1)} %param.24) | copy-start | bytes 3076
  85.7 6.6 %copy-start.56 = (f32[2048]{0:T(1024)}, f32[2048]{0:T(1024)S(1)}, u32[]{:S(2)}) copy-start(f32[2048]{0:T(1024)S(1)} %convert_element_type.212) | copy-start | bytes 24580
  86.0 1.7 copy-start.32
  87.7 6.8 %copy-start.59 = (f32[256]{0:T(256)}, f32[256]{0:T(256)S(1)}, u32[]{:S(2)}) copy-start(f32[256]{0:T(256)S(1)} %fusion.65) | copy-start | bytes 3076
  96.7 9.2 %copy-start.73 = (f32[32]{0:T(128)}, f32[32]{0:T(128)S(1)}, u32[]{:S(2)}) copy-start(f32[32]{0:T(128)S(1)} %multiply_exponential_fusion) | copy-start | bytes 388
  97.7 1.5 copy-start.50
  103.6 4.2 copy-start.71
  105.9 43.8 %copy-start.25 = (bf16[2048,352]{0,1:T(8,128)(2,1)S(1)}, bf16[2048,352]{0,1:T(8,128)(2,1)}, u32[]{:S(2)}) copy-start(bf16[2048,352]{0,1:T(8,128)(2,1)} %param.28) | copy-start | bytes 4325380
  151.0 2.4 copy-start.2
  151.0 2.4 copy-start.34
  151.0 2.5 copy-start.49
  154.1 1.4 copy-start.31
  165.0 261.4 %reduce-scatter.5.cloned.1.call-start = ((), (), s32[]{:S(2)}) async-start(), calls=%async_computation.10 | async-start | bytes 9437184 | tf_op jit(solution)/shard_map/reduce_scatter | solution.py:841
  256.9 2.2 copy-start.75
  256.9 2.7 copy-start.64
  262.3 5.6 copy-start.26
  262.3 5.6 copy-start.43
  268.0 1.4 copy-start.35
  268.0 1.4 copy-start.41
  348.0 19.9 %copy-start.47 = (pred[64,32,256]{2,1,0:T(32,128)(4,1)S(1)}, pred[64,32,256]{2,1,0:T(32,128)(4,1)}, u32[]{:S(2)}) copy-start(pred[64,32,256]{2,1,0:T(32,128)(4,1)} %iota_compare_fusion.7) | copy-start | bytes 1572868
  348.0 20.7 %copy-start.8 = (bf16[256,256]{1,0:T(8,128)(2,1)S(1)}, bf16[256,256]{1,0:T(8,128)(2,1)}, u32[]{:S(2)}) copy-start(bf16[256,256]{1,0:T(8,128)(2,1)} %fusion.28.dy_ref) | copy-start | bytes 393220
  348.1 20.7 %copy-start.11 = (f32[256,256]{1,0:T(8,128)S(1)}, f32[256,256]{1,0:T(8,128)}, u32[]{:S(2)}) copy-start(f32[256,256]{1,0:T(8,128)} %copy-done.10) | copy-start | bytes 786436
  348.1 20.7 %copy-start.13 = (f32[256,256]{1,0:T(8,128)S(1)}, f32[256,256]{1,0:T(8,128)}, u32[]{:S(2)}) copy-start(f32[256,256]{1,0:T(8,128)} %slice.119.shared_ref) | copy-start | bytes 786436
  348.1 20.7 %copy-start.19 = (f32[256,1]{1,0:T(8,128)S(1)}, f32[256,1]{1,0:T(8,128)}, u32[]{:S(2)}) copy-start(f32[256,1]{1,0:T(8,128)} %copy-done.18) | copy-start | bytes 3076
  348.1 38.5 %copy-start.28 = (bf16[256,2048]{1,0:T(8,128)(2,1)S(1)}, bf16[256,2048]{1,0:T(8,128)(2,1)}, u32[]{:S(2)}) copy-start(bf16[256,2048]{1,0:T(8,128)(2,1)} %param.26) | copy-start | bytes 3145732
  368.7 18.4 %copy-start.46 = (bf16[256,512]{0,1:T(8,128)(2,1)S(1)}, bf16[256,512]{0,1:T(8,128)(2,1)}, u32[]{:S(2)}) copy-start(bf16[256,512]{0,1:T(8,128)(2,1)} %copy.110) | copy-start | bytes 786436
  368.7 18.4 %copy-start.48 = (f32[2,256,256]{1,2,0:T(8,128)S(1)}, f32[2,256,256]{1,2,0:T(8,128)}, u32[]{:S(2)}) copy-start(f32[2,256,256]{1,2,0:T(8,128)} %get-tuple-element.152) | copy-start | bytes 1572868
  368.7 18.4 %copy-start.72 = (f32[2,256]{1,0:T(2,128)S(1)}, f32[2,256]{1,0:T(2,128)}, u32[]{:S(2)}) copy-start(f32[2,256]{1,0:T(2,128)} %copy-done.71) | copy-start | bytes 6148
  387.1 1.6 copy-start.53
  387.1 1.4 copy-start.54
  387.1 1.4 copy-start.57
  387.1 1.4 copy-start.58
  390.1 7.7 %copy-start.60 = (f32[256]{0:T(256)S(1)}, f32[256]{0:T(256)}, u32[]{:S(2)}) copy-start(f32[256]{0:T(256)} %copy-done.59) | copy-start | bytes 3076
  400.1 26.3 %all-to-all-start.4 = ((bf16[16,32,512]{2,1,0:T(8,128)(2,1)}), bf16[16,32,512]{2,1,0:T(8,128)(2,1)}, u32[]{:S(2)}, u32[]{:S(2)}) async-start(bf16[16,32,512]{2,1,0:T(8,128)(2,1)} %bitcast.141), calls=%async_computation.5 | async-start | bytes 1048576 | tf_op jit(solution)/shard_map/all_to_all | solution.py:895
  426.4 23.7 %all-to-all-start.1 = ((bf16[16,128,256]{2,1,0:T(8,128)(2,1)}), bf16[16,128,256]{2,1,0:T(8,128)(2,1)}, u32[]{:S(2)}, u32[]{:S(2)}) async-start(bf16[16,128,256]{2,1,0:T(8,128)(2,1)} %bitcast.143), calls=%async_computation.2 | async-start | bytes 2097152 | tf_op jit(solution)/shard_map/all_to_all | solution.py:842
  438.3 5.0 copy-start.4
  450.1 19.8 %all-to-all-start.5 = ((bf16[16,128,256]{2,1,0:T(8,128)(2,1)}), bf16[16,128,256]{2,1,0:T(8,128)(2,1)}, u32[]{:S(2)}, u32[]{:S(2)}) async-start(bf16[16,128,256]{2,1,0:T(8,128)(2,1)} %bitcast.138), calls=%async_computation.6 | async-start | bytes 2097152 | tf_op jit(solution)/shard_map/all_to_all | solution.py:895
  454.5 134.4 %all-gather.8.cloned.1.call-start = ((), (), s32[]{:S(2)}) async-start(), calls=%async_computation.11 | async-start | bytes 2228224 | tf_op jit(solution)/shard_map/all_gather | solution.py:851
  454.6 4.0 copy-start.30
  455.6 4.6 copy-start.38
  455.7 4.6 copy-start.6
  455.7 4.6 copy-start.12
  455.7 4.6 copy-start.29
  469.9 46.2 %all-to-all-start.2 = ((bf16[16,128,384]{2,1,0:T(8,128)(2,1)}), bf16[16,128,384]{2,1,0:T(8,128)(2,1)}, u32[]{:S(2)}, u32[]{:S(2)}) async-start(bf16[16,128,384]{2,1,0:T(8,128)(2,1)} %bitcast.142), calls=%async_computation.3 | async-start | bytes 3145728 | tf_op jit(solution)/shard_map/all_to_all | solution.py:895
  483.7 3.9 copy-start.33
  483.7 3.9 copy-start.39
  485.9 2.5 copy-start.14
  485.9 2.5 copy-start.17
  487.6 24.5 %copy-start.65 = (f32[256]{0:T(256)S(1)}, f32[256]{0:T(256)}, u32[]{:S(2)}) copy-start(f32[256]{0:T(256)} %copy-done.63) | copy-start | bytes 3076
  516.1 7.3 %copy-start.68 = (bf16[288]{0:T(512)(128)(2,1)S(1)}, bf16[288]{0:T(512)(128)(2,1)}, u32[]{:S(2)}) copy-start(bf16[288]{0:T(512)(128)(2,1)} %pad.10.clone) | copy-start | bytes 1732
  516.1 7.3 %copy-start.69 = (bf16[2,256]{1,0:T(2,128)(2,1)S(1)}, bf16[2,256]{1,0:T(2,128)(2,1)}, u32[]{:S(2)}) copy-start(bf16[2,256]{1,0:T(2,128)(2,1)} %convert_element_type.248) | copy-start | bytes 3076
  516.1 70.1 %all-to-all-start.3 = ((bf16[16,128,576]{1,2,0:T(8,128)(2,1)}), bf16[16,128,576]{1,2,0:T(8,128)(2,1)}, u32[]{:S(2)}, u32[]{:S(2)}) async-start(bf16[16,128,576]{1,2,0:T(8,128)(2,1)} %bitcast.131), calls=%async_computation.4 | async-start | bytes 4718592 | tf_op jit(solution)/shard_map/all_to_all | solution.py:895
  (25 other events, 21.9 us)
Sparse Core Ops, SparseCore 0:
  45.3 24.5 all-gather.3
  71.5 63.3 all-gather.5
  165.1 80.4 reduce-scatter.6
  257.1 77.5 reduce-scatter.4
  462.8 55.9 all-gather.7

commit v2 on v1

--- a/solution.py
+++ b/solution.py
@@ -260,33 +260,6 @@
     )(value)
 
 
-def rs_tensor_kernel(nch, in_ref, out_ref, *scratch):
-    rows = in_ref.shape[0]
-    width = in_ref.shape[1] // TENSOR
-    greet_x()
-
-    def emit(r, value):
-        out_ref[r] = value.astype(out_ref.dtype)
-
-    scatter_tensor(
-        nch, lambda r, owner: in_ref.at[r, cols(owner, width)], rows, width, emit, *scratch
-    )
-
-
-def rs_tensor(value, cid, nch=1, dtype=None):
-    rows, total = value.shape
-    width = total // TENSOR
-    return pl.pallas_call(
-        functools.partial(rs_tensor_kernel, nch),
-        out_shape=jax.ShapeDtypeStruct((rows, width), dtype or value.dtype),
-        in_specs=[ANY],
-        out_specs=VM,
-        scratch_shapes=scatter_scratch(nch, rows, width, value.dtype),
-        compiler_params=params(cid),
-        name="rs_tensor",
-    )(value)
-
-
 def middle_kernel(
     part_ref, x_ref, gain_ref, mid_ref, inv_ref, low_ref, full_ref, *scratch
 ):
@@ -326,46 +299,6 @@
         compiler_params=params(cid),
         name="middle_step",
     )(part, x_cols, gain)
-
-
-def back_middle_kernel(
-    routed_ref, shared_ref, mid_ref, inv_ref, gain_ref, dy_ref,
-    dmid_ref, dgain_ref, full_ref, low, buf, ssem, rsem, agss, agrs, lsem
-):
-    t = lax.axis_index("tensor")
-    greet_tensor()
-    dn = routed_ref[...] + shared_ref[...]
-    mid = mid_ref[...]
-    inv = inv_ref[...]
-    u = dn * gain_ref[...].astype(F32)
-    total = sum_rows_tensor(u * mid, buf, ssem, rsem)
-    dmid = dy_ref[...].astype(F32) + inv * u - mid * (inv * inv * inv * total * (1.0 / D))
-    dmid_ref[...] = dmid
-    low[...] = dmid.astype(BF16)
-    own = pltpu.make_async_copy(low, full_ref.at[:, cols(t, COLS)], lsem)
-    own.start()
-    dgain_ref[...] = jnp.sum(dn * mid * inv, axis=0, keepdims=True)
-    gather_tensor(1, low, full_ref, agss, agrs)
-    own.wait()
-
-
-def back_middle(routed, shared, mid, inv, gain, dy, cid):
-    return pl.pallas_call(
-        back_middle_kernel,
-        out_shape=(
-            jax.ShapeDtypeStruct((GROUP, COLS), F32),
-            jax.ShapeDtypeStruct((1, COLS), F32),
-            jax.ShapeDtypeStruct((GROUP, D), BF16),
-        ),
-        in_specs=[VM] * 6,
-        out_specs=(VM, VM, ANY),
-        scratch_shapes=[pltpu.VMEM((GROUP, COLS), BF16)]
-        + sum_rows_scratch()
-        + gather_sems(1)
-        + [DMA],
-        compiler_params=params(cid),
-        name="back_middle",
-    )(routed, shared, mid, inv, gain, dy)
 
 
 def back_input_kernel(
@@ -463,45 +396,6 @@
         name="ar_tensor",
     )(value.reshape(TENSOR, part, n))
     return out.reshape(rows, n)
-
-
-def a2a_expert_kernel(in_ref, out_ref, ssem, rsem, lsem):
-    e = lax.axis_index("expert")
-    z = e // YN
-    y = lax.rem(e, YN)
-    peers = []
-    for dz in range(ZN):
-        for dy in range(YN):
-            if dz or dy:
-                to = lax.rem(z + dz, ZN) * YN + lax.rem(y + dy, YN)
-                frm = lax.rem(z + ZN - dz, ZN) * YN + lax.rem(y + YN - dy, YN)
-                peers.append((to, frm))
-    greet([("expert", to) for to, frm in peers])
-    own = pltpu.make_async_copy(in_ref.at[e], out_ref.at[e], lsem)
-    own.start()
-    sends = []
-    for j, (to, frm) in enumerate(peers):
-        c = remote(in_ref.at[to], out_ref.at[e], ssem.at[j], rsem.at[j], "expert", to)
-        c.start()
-        sends.append(c)
-    for j, (to, frm) in enumerate(peers):
-        remote(out_ref.at[frm], out_ref.at[frm], ssem.at[j], rsem.at[j], "expert", to).wait_recv()
-    for s in sends:
-        s.wait_send()
-    own.wait()
-
-
-def a2a_expert(value, cid):
-    n = value.shape[0]
-    return pl.pallas_call(
-        a2a_expert_kernel,
-        out_shape=jax.ShapeDtypeStruct(value.shape, value.dtype),
-        in_specs=[ANY],
-        out_specs=ANY,
-        scratch_shapes=[DMA((n - 1,)), DMA((n - 1,)), DMA],
-        compiler_params=params(cid),
-        name="a2a_expert",
-    )(value)
 
 
 def ag_expert_kernel(a_ref, b_ref, ao_ref, bo_ref, ssem, rsem, lsem):
@@ -601,50 +495,399 @@
     return lax.dot_general(a, b, (((0,), (0,)), ((), ())), preferred_element_type=F32)
 
 
-def expert_kernel(rows_ref, grad_ref, wg_ref, wu_ref, wd_ref, part_ref, drows_ref, gg_ref, gu_ref, gd_ref):
-    n = GROUPS * PADCAP
-    rows = rows_ref[...].reshape(n, D)
-    grad = grad_ref[...].reshape(n, D)
-    wg, wu, wd = wg_ref[0], wu_ref[0], wd_ref[0]
-    gate = dot_nt(rows, wg)
-    up = dot_nt(rows, wu)
-    sig = jax.nn.sigmoid(gate)
-    silu = gate * sig
-    hidden = (silu * up).astype(BF16)
-    part_ref[...] = dot_nn(hidden, wd).astype(BF16).reshape(part_ref.shape)
-    gd_ref[0] = dot_tn(hidden, grad)
-    dh = dot_nt(grad, wd)
-    dg = (dh * up * (sig * (1.0 + gate * (1.0 - sig)))).astype(BF16)
-    du = (dh * silu).astype(BF16)
-    gg_ref[0] = dot_tn(dg, rows)
-    gu_ref[0] = dot_tn(du, rows)
-    drows_ref[...] = (dot_nn(dg, wg) + dot_nn(du, wu)).astype(BF16).reshape(drows_ref.shape)
-
-
-def expert_step(rows, grads, wg, wu, wd):
+ROWS = GROUPS * PADCAP
+
+
+def expert_peers():
+    e = lax.axis_index("expert")
+    z = e // YN
+    y = lax.rem(e, YN)
+    peers = []
+    for dz in range(ZN):
+        for dy in range(YN):
+            if dz or dy:
+                to = lax.rem(z + dz, ZN) * YN + lax.rem(y + dy, YN)
+                frm = lax.rem(z + ZN - dz, ZN) * YN + lax.rem(y + YN - dy, YN)
+                peers.append((to, frm))
+    return e, peers
+
+
+def seat_rows(index):
+    return pl.ds(pl.multiple_of(index * PADCAP, PADCAP), PADCAP)
+
+
+def moe_kernel(
+    place_ref, ncols_ref, nfull_hbm, dy_hbm, sg_hbm, su_hbm, sd_hbm, wg_hbm, wu_hbm, wd_hbm, grads_hbm,
+    mid_ref, inv_ref, gain_ref, dyc_ref,
+    part_hbm, gg_hbm, gu_hbm, gd_hbm, shout_ref, sh_ref, dsg_ref, dsu_ref, dmid_ref, dgain_ref, dattn_hbm,
+    nfull, dyf, sgv, suv, sdv, outbuf, rows, drows, sib, half, full, wbuf, gbuf, gout, pbuf, res, back, shsum, low,
+    d_s, d_r, a_s, a_r, r_s, r_r, b_s, b_r, f_s, f_r, st_buf, st_s, st_r, l_in, l_w, l_g, l_out, l_own,
+):
+    t, right, left, far, twin = x_peers()
+    flip = twin - t
+    e, peers = expert_peers()
+    greet(
+        [("tensor", lax.rem(t + j, TENSOR)) for j in range(1, TENSOR)]
+        + [("expert", to) for to, frm in peers]
+    )
+    sends = []
+
+    def send(src, dst, ssem, rsem, axis, to):
+        c = remote(src, dst, ssem, rsem, axis, to)
+        c.start()
+        sends.append(c)
+
+    def got(ref, ssem, rsem):
+        remote(ref, ref, ssem, rsem, "tensor", twin).wait_recv()
+
+    early = [
+        pltpu.make_async_copy(src, dst, l_in.at[i])
+        for i, (src, dst) in enumerate(
+            [(nfull_hbm, nfull), (sg_hbm, sgv), (su_hbm, suv), (sd_hbm, sdv), (dy_hbm, dyf)]
+        )
+    ]
+    for c in early:
+        c.start()
+
+    def load(k):
+        s = k % 2
+        copies = [
+            pltpu.make_async_copy(ref.at[k], wbuf.at[s, i], l_w.at[s, i])
+            for i, ref in enumerate((wg_hbm, wu_hbm, wd_hbm))
+        ]
+        copies.append(pltpu.make_async_copy(grads_hbm.at[k], gbuf.at[s], l_g.at[s]))
+        for c in copies:
+            c.start()
+        return copies
+
+    loads = {0: load(0), 1: load(1)}
+
+    own_copies = []
+    for k in range(LOCAL):
+        outbuf[k] = dot_nn(place_ref[k], ncols_ref[...]).astype(BF16)
+        c = pltpu.make_async_copy(
+            outbuf.at[k, seat_rows(e)], rows.at[k, seat_rows(e), cols(t, COLS)], l_own.at[k]
+        )
+        c.start()
+        own_copies.append(c)
+        for j, (to, frm) in enumerate(peers):
+            send(
+                outbuf.at[k, seat_rows(to)], rows.at[k, seat_rows(e), cols(t, COLS)],
+                d_s.at[k, j], d_r.at[k, j], "expert", to,
+            )
+
+    h = ROWS // 2
+
+    def block(k, owner, part=None):
+        if part is None:
+            return rows.at[k, :, cols(owner, COLS)]
+        return rows.at[k, pl.ds(part * h, h), cols(owner, COLS)]
+
+    def asend(k, j, ref, to):
+        send(ref, ref, a_s.at[k, j], a_r.at[k, j], "tensor", to)
+
+    def agot(k, j, ref):
+        got(ref, a_s.at[k, j], a_r.at[k, j])
+
+    def gather_1(k):
+        own_copies[k].wait()
+        for j, (to, frm) in enumerate(peers):
+            ref = rows.at[k, seat_rows(frm), cols(t, COLS)]
+            got(ref, d_s.at[k, j], d_r.at[k, j])
+        asend(k, 0, block(k, t), right)
+        asend(k, 1, block(k, t), left)
+        asend(k, 4, block(k, t), twin)
+
+    def gather_2(k):
+        agot(k, 0, block(k, left))
+        asend(k, 2, block(k, left, 0), right)
+        asend(k, 5, block(k, left), twin)
+        agot(k, 1, block(k, right))
+        asend(k, 3, block(k, right, 1), left)
+        asend(k, 6, block(k, right), twin)
+
+    def gather_3(k):
+        agot(k, 2, block(k, far, 0))
+        asend(k, 7, block(k, far, 0), twin)
+        agot(k, 3, block(k, far, 1))
+        asend(k, 8, block(k, far, 1), twin)
+
+    def gather_4(k):
+        agot(k, 4, block(k, twin))
+        agot(k, 5, block(k, left + flip))
+        agot(k, 6, block(k, right + flip))
+        agot(k, 7, block(k, far + flip, 0))
+        agot(k, 8, block(k, far + flip, 1))
+
+    order = (far, right, left, t)
+
+    def slot(k):
+        return 3 if k == LOCAL else k % 3
+
+    def rsend(k, j, src, dst, to):
+        send(src, dst, r_s.at[k, j], r_r.at[k, j], "tensor", to)
+
+    def rgot(k, j, ref):
+        got(ref, r_s.at[k, j], r_r.at[k, j])
+
+    def mine(k, j):
+        return drows[slot(k), :, cols(order[j], COLS)].astype(F32)
+
+    twin_sends = {}
+
+    def sum_1(k):
+        first = len(sends)
+        for j, owner in enumerate(order):
+            rsend(k, j, drows.at[slot(k), :, cols(owner + flip, COLS)], sib.at[k, j], twin)
+        twin_sends[k] = sends[first:]
+        del sends[first:]
+
+    def sum_2(k):
+        rgot(k, 0, sib.at[k, 0])
+        sib[k, 0] = (mine(k, 0) + sib[k, 0].astype(F32)).astype(BF16)
+        rsend(k, 4, sib.at[k, 0, pl.ds(0, h)], half.at[k, 0], right)
+        rsend(k, 5, sib.at[k, 0, pl.ds(h, h)], half.at[k, 1], left)
+
+    def sum_3(k):
+        for j, to in ((1, right), (2, left)):
+            rgot(k, j, sib.at[k, j])
+            rgot(k, 3 + j, half.at[k, j - 1])
+            both = mine(k, j) + sib[k, j].astype(F32)
+            extra = half[k, j - 1].astype(F32)
+            if j == 1:
+                sib[k, j, :h] = (both[:h] + extra).astype(BF16)
+                sib[k, j, h:] = both[h:].astype(BF16)
+            else:
+                sib[k, j, :h] = both[:h].astype(BF16)
+                sib[k, j, h:] = (both[h:] + extra).astype(BF16)
+            rsend(k, 5 + j, sib.at[k, j], full.at[k, j - 1], to)
+
+    def sum_4(k):
+        rgot(k, 3, sib.at[k, 3])
+        rgot(k, 6, full.at[k, 0])
+        rgot(k, 7, full.at[k, 1])
+        value = mine(k, 3) + sib[k, 3].astype(F32) + full[k, 0].astype(F32) + full[k, 1].astype(F32)
+        for c in twin_sends[k]:
+            c.wait_send()
+        if k == LOCAL:
+            shsum[...] = value
+            return
+        res[k] = value.astype(BF16)
+        c = pltpu.make_async_copy(res.at[k, seat_rows(e)], back.at[k, seat_rows(e)], l_own.at[k])
+        c.start()
+        own_copies[k] = c
+        for j, (to, frm) in enumerate(peers):
+            send(res.at[k, seat_rows(to)], back.at[k, seat_rows(e)], b_s.at[k, j], b_r.at[k, j], "expert", to)
+
+    def shared_forward():
+        for c in early[:4]:
+            c.wait()
+        n = nfull[...]
+        g = dot_nt(n, sgv[...])
+        u = dot_nt(n, suv[...])
+        sig = jax.nn.sigmoid(g)
+        silu = g * sig
+        sh_ref[...] = (silu * u).astype(BF16)
+        return g, u, sig, silu
+
+    def shared_backward(g, u, sig, silu):
+        early[4].wait()
+        dh = dot_nt(dyf[...], sdv[...])
+        dsg_ref[...] = (dh * u * (sig * (1.0 + g * (1.0 - sig)))).astype(BF16)
+        dsu_ref[...] = (dh * silu).astype(BF16)
+
+    tiles = [pl.ds(i * 512, 512) for i in range(D // 512)]
+
+    def shared_rows():
+        hid = sh_ref[...]
+        dsg, dsu = dsg_ref[...], dsu_ref[...]
+        for n in tiles:
+            drows[3, :GROUP, n] = dot_nn(hid, sdv[:, n]).astype(BF16)
+            drows[3, GROUP:, n] = (dot_nn(dsg, sgv[:, n]) + dot_nn(dsu, suv[:, n])).astype(BF16)
+
+    out_copies = {}
+
+    def compute_1(k):
+        s = k % 2
+        for c in loads[k]:
+            c.wait()
+        r = rows[k]
+        gate = dot_nt(r, wbuf[s, 0])
+        up = dot_nt(r, wbuf[s, 1])
+        dh = dot_nt(gbuf[s], wbuf[s, 2])
+        sig = jax.nn.sigmoid(gate)
+        silu = gate * sig
+        hidden = (silu * up).astype(BF16)
+        dg = (dh * up * (sig * (1.0 + gate * (1.0 - sig)))).astype(BF16)
+        du = (dh * silu).astype(BF16)
+        for n in tiles:
+            drows[slot(k), :, n] = (
+                dot_nn(dg, wbuf[s, 0, :, n]) + dot_nn(du, wbuf[s, 1, :, n])
+            ).astype(BF16)
+        return hidden, dg, du
+
+    def compute_2(k, hidden, dg, du):
+        s = k % 2
+        if k:
+            for c in out_copies[k - 1]:
+                c.wait()
+        for n in tiles:
+            pbuf[:, n] = dot_nn(hidden, wbuf[s, 2, :, n]).astype(BF16)
+            gout[0, :, n] = dot_tn(dg, rows[k, :, n])
+            gout[1, :, n] = dot_tn(du, rows[k, :, n])
+            gout[2, :, n] = dot_tn(hidden, gbuf[s, :, n])
+        out_copies[k] = [
+            pltpu.make_async_copy(src, dst.at[k], l_out.at[i])
+            for i, (src, dst) in enumerate(
+                [(pbuf, part_hbm), (gout.at[0], gg_hbm), (gout.at[1], gu_hbm), (gout.at[2], gd_hbm)]
+            )
+        ]
+        for c in out_copies[k]:
+            c.start()
+        if k + 2 < LOCAL:
+            loads[k + 2] = load(k + 2)
+
+    state = shared_forward()
+    gather_1(0)
+    shared_backward(*state)
+    gather_1(1)
+    gather_2(0)
+    shared_rows()
+    sum_1(4)
+    gather_1(2)
+    gather_2(1)
+    gather_3(0)
+    gather_1(3)
+    gather_4(0)
+    c0 = compute_1(0)
+    sum_1(0)
+    gather_2(2)
+    gather_3(1)
+    sum_2(4)
+    compute_2(0, *c0)
+    gather_4(1)
+    sum_2(0)
+    c1 = compute_1(1)
+    sum_1(1)
+    gather_2(3)
+    gather_3(2)
+    sum_3(0)
+    compute_2(1, *c1)
+    gather_4(2)
+    sum_2(1)
+    c2 = compute_1(2)
+    sum_1(2)
+    gather_3(3)
+    sum_3(1)
+    sum_4(0)
+    sum_3(4)
+    compute_2(2, *c2)
+    gather_4(3)
+    sum_2(2)
+    c3 = compute_1(3)
+    sum_1(3)
+    sum_3(2)
+    sum_4(1)
+    sum_2(3)
+    compute_2(3, *c3)
+    sum_4(2)
+    sum_3(3)
+    sum_4(4)
+    shout_ref[...] = shsum[:GROUP]
+    sum_4(3)
+
+    dn = shsum[GROUP:]
+    for k in range(LOCAL):
+        own_copies[k].wait()
+        for j, (to, frm) in enumerate(peers):
+            got(back.at[k, seat_rows(frm)], b_s.at[k, j], b_r.at[k, j])
+        dn = dn + dot_tn(place_ref[k], back[k])
+
+    mid = mid_ref[...]
+    inv = inv_ref[...]
+    u = dn * gain_ref[...].astype(F32)
+    total = sum_rows_tensor(u * mid, st_buf, st_s, st_r)
+    dmid = dyc_ref[...].astype(F32) + inv * u - mid * (inv * inv * inv * total * (1.0 / D))
+    dmid_ref[...] = dmid
+    low[...] = dmid.astype(BF16)
+    own = pltpu.make_async_copy(low, dattn_hbm.at[:, cols(t, COLS)], l_own.at[0])
+    own.start()
+    dgain_ref[...] = jnp.sum(dn * mid * inv, axis=0, keepdims=True)
+    gather_tensor(1, low, dattn_hbm, f_s, f_r)
+    own.wait()
+    for c in out_copies[LOCAL - 1]:
+        c.wait()
+    for c in sends:
+        c.wait_send()
+
+
+def moe_step(place, ncols, nfull, dy, sg, su, sd, wg, wu, wd, grads, mid, inv, gain, dyc, cid):
     hid = wd.shape[1]
-    block = pl.BlockSpec((GROUPS, 1, PADCAP, D), lambda i: (0, i, 0, 0))
-    weight = pl.BlockSpec((1, hid, D), lambda i: (i, 0, 0))
-    shape = jax.ShapeDtypeStruct((GROUPS, LOCAL, PADCAP, D), BF16)
+    wide = sd.shape[0]
     wshape = jax.ShapeDtypeStruct((LOCAL, hid, D), F32)
+    vmem = pltpu.VMEM
     return pl.pallas_call(
-        expert_kernel,
-        grid=(LOCAL,),
-        out_shape=(shape, shape, wshape, wshape, wshape),
-        in_specs=[block, block, weight, weight, weight],
-        out_specs=(block, block, weight, weight, weight),
-        compiler_params=pltpu.CompilerParams(vmem_limit_bytes=60 * MIB),
+        moe_kernel,
+        out_shape=(
+            jax.ShapeDtypeStruct((LOCAL, ROWS, D), BF16),
+            wshape,
+            wshape,
+            wshape,
+            jax.ShapeDtypeStruct((GROUP, COLS), F32),
+            jax.ShapeDtypeStruct((GROUP, wide), BF16),
+            jax.ShapeDtypeStruct((GROUP, wide), BF16),
+            jax.ShapeDtypeStruct((GROUP, wide), BF16),
+            jax.ShapeDtypeStruct((GROUP, COLS), F32),
+            jax.ShapeDtypeStruct((1, COLS), F32),
+            jax.ShapeDtypeStruct((GROUP, D), BF16),
+        ),
+        in_specs=[VM, VM] + [ANY] * 9 + [VM] * 4,
+        out_specs=(ANY, ANY, ANY, ANY, VM, VM, VM, VM, VM, VM, ANY),
+        scratch_shapes=[
+            vmem((GROUP, D), BF16),
+            vmem((GROUP, D), BF16),
+            vmem((wide, D), BF16),
+            vmem((wide, D), BF16),
+            vmem((wide, D), BF16),
+            vmem((LOCAL, ROWS, COLS), BF16),
+            vmem((LOCAL, ROWS, D), BF16),
+            vmem((4, ROWS, D), BF16),
+            vmem((LOCAL + 1, 4, ROWS, COLS), BF16),
+            vmem((LOCAL + 1, 2, ROWS // 2, COLS), BF16),
+            vmem((LOCAL + 1, 2, ROWS, COLS), BF16),
+            vmem((2, 3, hid, D), BF16),
+            vmem((2, ROWS, D), BF16),
+            vmem((3, hid, D), F32),
+            vmem((ROWS, D), BF16),
+            vmem((LOCAL, ROWS, COLS), BF16),
+            vmem((LOCAL, ROWS, COLS), BF16),
+            vmem((2 * GROUP, COLS), F32),
+            vmem((GROUP, COLS), BF16),
+            DMA((LOCAL, 15)),
+            DMA((LOCAL, 15)),
+            DMA((LOCAL, 9)),
+            DMA((LOCAL, 9)),
+            DMA((LOCAL + 1, 8)),
+            DMA((LOCAL + 1, 8)),
+            DMA((LOCAL, 15)),
+            DMA((LOCAL, 15)),
+            DMA((1, 9)),
+            DMA((1, 9)),
+            vmem((TENSOR, 8, GROUP), F32),
+            DMA((TENSOR,)),
+            DMA((TENSOR,)),
+            DMA((5,)),
+            DMA((2, 3)),
+            DMA((2,)),
+            DMA((4,)),
+            DMA((LOCAL,)),
+        ],
+        compiler_params=params(cid, 63),
         cost_estimate=pl.CostEstimate(
-            flops=9 * 2 * 2048 * 2048 * hid, bytes_accessed=60 * MIB, transcendentals=0
+            flops=40 * 10**9, bytes_accessed=100 * MIB, transcendentals=0
         ),
-        name="expert_step",
-    )(
-        rows.reshape(GROUPS, LOCAL, PADCAP, D),
-        grads.reshape(GROUPS, LOCAL, PADCAP, D),
-        wg,
-        wu,
-        wd,
-    )
+        name="moe_step",
+    )(place, ncols, nfull, dy, sg, su, sd, wg, wu, wd, grads, mid, inv, gain, dyc)
 
 
 def rms_scale(value, gain):
@@ -726,7 +969,8 @@
 
     chosen = routes.T
     gates = gate_weights.T
-    experts = jnp.arange(EXPERTS, dtype=jnp.int32)
+    numbers = jnp.arange(EXPERTS, dtype=jnp.int32)
+    experts = lax.rem(numbers, GROUPS) * LOCAL + numbers // GROUPS
     hit = chosen[:, None, :] == experts[None, :, None]
     member = jnp.sum(hit.astype(F32), axis=0)
     gate_of = jnp.sum(jnp.where(hit, gates[:, None, :], 0.0), axis=0)
@@ -745,8 +989,8 @@
     weight_high = weight_high.astype(BF16)
 
     slot_grad = (slot_gate * dot_nn(place, dy_cols)).astype(BF16)
-    slot_grad = slot_grad.reshape(GROUPS, LOCAL * PADCAP, COLS)
-    slot_grad = lax.all_to_all(slot_grad, "expert", split_axis=0, concat_axis=0, tiled=True)
+    slot_grad = slot_grad.reshape(LOCAL, GROUPS, PADCAP, COLS)
+    slot_grad = lax.all_to_all(slot_grad, "expert", split_axis=1, concat_axis=1, tiled=True)
     grad_rows = lax.all_gather(slot_grad.reshape(-1, COLS), "tensor", axis=1, tiled=True)
 
     attn_gainf = attn_gain.astype(F32)
@@ -793,24 +1037,26 @@
         attn_part, x_cols, own_cols(ffn_gain), 2
     )
 
-    outgoing = dot_nn(place, normed_two_cols).astype(BF16)
-    received = a2a_expert(outgoing.reshape(GROUPS, LOCAL * PADCAP, COLS), 3)
-    rows = ag_tensor(received.reshape(-1, COLS), 4, 4)
-
-    sg_t, su_t = shared_gate.T, shared_up.T
-    shared_g = dot_nt(normed_two, sg_t)
-    shared_u = dot_nt(normed_two, su_t)
-    shared_sig = jax.nn.sigmoid(shared_g)
-    shared_silu = shared_g * shared_sig
-    shared_h = (shared_silu * shared_u).astype(BF16)
-    shared_part = dot_nn(shared_h, shared_down).astype(BF16)
-    grad_sh = dot_nt(dy_full, shared_down)
-    grad_sg = (
-        grad_sh * shared_u * (shared_sig * (1.0 + shared_g * (1.0 - shared_sig)))
-    ).astype(BF16)
-    grad_su = (grad_sh * shared_silu).astype(BF16)
-    shared_grad = (dot_nn(grad_sg, sg_t) + dot_nn(grad_su, su_t)).astype(BF16)
-    shared_sum = rs_tensor(jnp.concatenate([shared_part, shared_grad], axis=0), 5, 1, F32)
+    (
+        part, grad_eg, grad_eu, grad_ed, shared_out, shared_h, grad_sg, grad_su, dmid, dgain_ffn, d_attn
+    ) = moe_step(
+        place.reshape(LOCAL, ROWS, GROUP),
+        normed_two_cols,
+        normed_two,
+        dy_full,
+        shared_gate.T,
+        shared_up.T,
+        shared_down,
+        jnp.swapaxes(expert_gate, 1, 2),
+        jnp.swapaxes(expert_up, 1, 2),
+        expert_down,
+        grad_rows.reshape(LOCAL, ROWS, D),
+        middle,
+        inv_two,
+        own_cols(ffn_gain),
+        dy_cols,
+        3,
+    )
     shared_weights = jnp.concatenate(
         [
             dot_tn(normed_two, grad_sg).astype(BF16),
@@ -822,37 +1068,22 @@
     shared_weights = lax.psum_scatter(
         shared_weights, "expert", scatter_dimension=0, tiled=True
     ).astype(F32)
-    wide = shared_g.shape[1]
+    wide = shared_h.shape[1]
     grad_sgate = shared_weights[:, :wide]
     grad_sup = shared_weights[:, wide : 2 * wide]
     grad_sdown = shared_weights[:, 2 * wide :].T
 
-    part, drows, grad_eg, grad_eu, grad_ed = expert_step(
-        rows,
-        grad_rows,
-        jnp.swapaxes(expert_gate, 1, 2),
-        jnp.swapaxes(expert_up, 1, 2),
-        expert_down,
-    )
-    back = rs_tensor(drows.reshape(-1, D), 6, 4)
-    back = a2a_expert(back.reshape(GROUPS, LOCAL * PADCAP, COLS), 7)
-    routed_grad = dot_tn(place, back.reshape(-1, COLS))
-
     returned = lax.psum_scatter(part.reshape(-1, D), "tensor", scatter_dimension=1, tiled=True)
     returned = lax.all_to_all(
-        returned.reshape(GROUPS, LOCAL * PADCAP, COLS),
+        returned.reshape(LOCAL, GROUPS, PADCAP, COLS),
         "expert",
-        split_axis=0,
-        concat_axis=0,
+        split_axis=1,
+        concat_axis=1,
         tiled=True,
     ).reshape(-1, COLS)
     routed = dot_tn(weight_high, returned) + dot_tn(weight_low, returned)
-    output_cols = (middle + shared_sum[:GROUP] + routed).astype(BF16)
+    output_cols = (middle + shared_out + routed).astype(BF16)
     all_out = lax.all_gather(output_cols, "expert", axis=0, tiled=True)
-
-    dmid, dgain_ffn, d_attn = back_middle(
-        routed_grad, shared_sum[GROUP:], middle, inv_two, own_cols(ffn_gain), dy_cols, 8
-    )
 
     grad_wout = dot_tn(d_attn, mixed).astype(BF16)
     grad_mixed = dot_nt(d_attn, w_out).astype(BF16).reshape(GROUP, heads, VDIM)

time: 607 us -> 524 us (0.86)
  Pallas kernels: 366 us -> 302 us
  waiting for transfers between devices: 11.7 us -> 43.5 us
  other arithmetic: 44.5 us -> 19.1 us
  matrix products: 54.1 us -> 32.8 us
    pallas_call x2 -> x1, Pallas kernels: 55 us -> 14.2 us  [ag_tensor(): pl.pallas_call(functools.partial(ag_tensor_kernel, nch), out_shape=jax.Sh...]
    pallas_call x6 -> x1, Pallas kernels: 158 us -> 118 us  [moe_step(): pl.pallas_call(moe_kernel, out_shape=(jax.ShapeDtypeStruct((LOCAL, ROWS,...]
    reduce_scatter x1, waiting for transfers between devices: 0.01 us -> 14.7 us  [per_device(): lax.psum_scatter(part.reshape(-1, D), 'tensor', scatter_dimension=1, tile...]
    all_gather x1, waiting for transfers between devices: 0.01 us -> 8.57 us  [per_device(): all_out = lax.all_gather(output_cols, 'expert', axis=0, tiled=True)]
    dot_general x15 -> x11, matrix products: 20.8 us -> 13.3 us  [dot_nn(): lax.dot_general(a, b, (((1,), (0,)), ((), ())), preferred_element_type=F32)]
    all_to_all x4, waiting for transfers between devices: 7.17 us -> 13.8 us  [sum_groups(): lax.all_to_all(value, 'expert', split_axis=0, concat_axis=0, tiled=True)]
    unnamed x166 -> x163, local copies, waits for them, and re-layouts: 30 us -> 35.6 us
    dot_general x10 -> x9, matrix products: 15.8 us -> 10.6 us  [dot_tn(): lax.dot_general(a, b, (((0,), (0,)), ((), ())), preferred_element_type=F32)]
  transfers between devices with their start and end apart: 10 -> 10, of which waited for: 2 -> 4; matrix products, arithmetic and copies ran while one was open for 23% -> 15% of each run, Pallas kernels for 56% -> 30%
where the time goes in v2:
time: 524 us; the launch traced here: 515 us
  Pallas kernels  302 us (58%)
  local copies, waits for them, and re-layouts  54.2 us (10%)
  waiting for transfers between devices  43.5 us (8%)
  matrix products  32.8 us (6%)
  starting transfers between devices  27.7 us (5%)
  blocking collectives  19.8 us (4%)
  other arithmetic  19.1 us (4%)
  between operations  15.6 us (3%)
    pallas_call x1, Pallas kernels, moe_step(): pl.pallas_call(moe_kernel, out_shape=(jax.ShapeDtypeStruct((LOCAL, ROWS,...  118 us
    pallas_call x2, Pallas kernels, ag_expert(): pl.pallas_call(ag_expert_kernel, out_shape=(shape, shape), in_specs=[ANY,...  81.8 us
    pallas_call x1, Pallas kernels, middle_step(): pl.pallas_call(middle_kernel, out_shape=(jax.ShapeDtypeStruct((GROUP, COL...  43.3 us
    unnamed x163, local copies, waits for them, and re-layouts  35.6 us
    pallas_call x1, Pallas kernels, back_input(): pl.pallas_call(back_input_kernel, out_shape=(jax.ShapeDtypeStruct((GROUP,...  25.8 us
    all_to_all x4, starting transfers between devices, sum_groups(): lax.all_to_all(value, 'expert', split_axis=0, concat_axis=0, tiled=True)  20.5 us
    all_to_all x1, blocking collectives, per_device(): lax.all_to_all(slot_grad, 'expert', split_axis=1, concat_axis=1, tiled=True)  19.8 us
    pallas_call x1, Pallas kernels, ar_tensor(): pl.pallas_call(ar_kernel, out_shape=jax.ShapeDtypeStruct((TENSOR, part, n...  19 us
  transfers between devices with their start and end apart: 10, of which 4 were waited for; matrix products, arithmetic and copies ran while one was open for 15% of the time, Pallas kernels for 30%

profile of v2, /device:TPU:1, one launch (start us, length us, event | category | flops | bytes accessed | tf_op | source)
XLA Modules:
  0.0 514.9 jit_solution(9198883309907181376)
XLA Ops:
  8.1 1.4 select_reduce_fusion.8
  9.9 0.9 copy-done.8
  10.8 0.9 copy-done.9
  11.7 29.5 %ag_expert.2 = (bf16[4,4,256,256]{3,2,1,0:T(8,128)(2,1)S(1)}, bf16[4,4,256,256]{3,2,1,0:T(8,128)(2,1)S(1)}) custom-call(bf16[256,256]{1,0:T(8,128)(2,1)S(1)} %copy-done.8, bf16[256,256]{1,0:T(8,128)(2,1)S(1)} %copy-done.9), custom_call_target="tpu_custom_call" | custom-call | tf_op jit(solution)/shard_map/ag_expert/pallas_call | solution.py:474
  41.2 1.4 fusion.28.dyc_ref
  43.0 1.7 fusion.11
  45.9 19.8 %all_to_all.46 = bf16[4,16,32,256]{3,2,0,1:T(8,128)(2,1)S(1)} all-to-all(bf16[4,16,32,256]{3,2,0,1:T(8,128)(2,1)S(1)} %copy.110), channel_id=1, replica_groups=mesh['expert'=16,'tensor'=8] {'expert'}, dimensions={1} | all-to-all | bytes 2097152 | tf_op jit(solution)/shard_map/all_to_all | solution.py:993
  65.7 1.1 copy.111
  67.7 14.2 %ag_tensor.1 = bf16[256,2048]{1,0:T(8,128)(2,1)S(1)} custom-call(bf16[256,256]{1,0:T(8,128)(2,1)S(1)} %fusion.27.in_ref.x_ref), custom_call_target="tpu_custom_call" | custom-call | tf_op jit(solution)/shard_map/ag_tensor/pallas_call | solution.py:252
  82.3 0.9 fusion.84
  84.0 2.3 fusion.82
  87.7 1.2 fusion.89
  88.9 1.5 convolution_convert_fusion.10
  90.9 43.3 %middle_step.1 = (f32[256,256]{1,0:T(8,128)S(1)}, f32[256,1]{1,0:T(8,128)S(1)}, bf16[256,256]{1,0:T(8,128)(2,1)S(1)}, bf16[256,2048]{1,0:T(8,128)(2,1)S(1)}) custom-call(f32[256,2048]{1,0:T(8,128)S(1)} %fusion.90.part_ref, bf16[256,256]{1,0:T(8,128)(2,1)S(1)} %fusion.27.in_ref.x_ref, bf16[1,256]{1,0:T(2,128)(2,1)S(1)} %reshape.444.gain_ref), custom_call_target="tpu_custom_call" | custom-call | tf_op jit(solution)/shard_map/middle_step/pallas_call | solution.py:285
  134.3 1.0 copy-done.3
  137.4 1.2 fusion.17.place_ref
  138.6 118.1 %moe_step.1 = (bf16[4,512,2048]{2,1,0:T(8,128)(2,1)}, f32[4,176,2048]{2,1,0:T(8,128)}, f32[4,176,2048]{2,1,0:T(8,128)}, f32[4,176,2048]{2,1,0:T(8,128)}, f32[256...) custom-call(bf16[4,512,256]{2,1,0:T(8,128)(2,1)} %fusion.17.place_re, ...), custom_call_target="tpu_custom_call" | custom-call | flops 40000000000 | bytes 104857600 | tf_op jit(solution)/shard_map/moe_step/pallas_call | solution.py:829
  256.8 1.1 copy-done.4
  259.8 2.3 pad_maximum_fusion
  262.1 6.5 %copy.135 = bf16[2048,1056]{1,0:T(8,128)(2,1)} copy(bf16[2048,1056]{0,1:T(8,128)(2,1)} %pad_maximum_fusion) | data formatting | bytes 8650752
  272.2 1.6 convolution_bitcast_fusion
  273.9 1.2 convolution_convert_fusion.7
  275.0 4.7 all-to-all-start.4
  280.6 19.0 %ar_tensor.1 = bf16[8,32,640]{2,1,0:T(8,128)(2,1)S(1)} custom-call(bf16[8,32,640]{2,1,0:T(8,128)(2,1)S(1)} %maximum_maximum_fusion.in_ref), custom_call_target="tpu_custom_call" | custom-call | tf_op jit(solution)/shard_map/ar_tensor/pallas_call | solution.py:385
  299.6 14.7 %reduce-scatter.5.cloned.1.call-done = bf16[2048,256]{1,0:T(8,128)(2,1)} async-done(((bf16[2048,2048]{1,0:T(8,128)(2,1)}), bf16[2048,256]{1,0:T(8,128)(2,1)}) %reduce-scatter.5.cloned.1.call-update) | async-done | bytes 1048592 | tf_op jit(solution)/shard_map/reduce_scatter | solution.py:1076
  314.3 2.3 copy.112
  316.6 6.8 %all-to-all-start.1 = ((bf16[4,16,32,256]{3,2,0,1:T(8,128)(2,1)}), bf16[4,16,32,256]{3,2,0,1:T(8,128)(2,1)}, u32[]{:S(2)}, u32[]{:S(2)}) async-start(bf16[4,16,32,256]{3,2,0,1:T(8,128)(2,1)} %copy.112), calls=%async_computation.2 | async-start | bytes 2097152 | tf_op jit(solution)/shard_map/all_to_all | solution.py:1077
  323.4 0.8 copy-done.22
  324.3 0.9 slice.147
  325.2 1.2 copy.138
  326.4 1.7 fusion.86
  328.1 1.0 copy.139
  329.8 1.2 fusion.23
  331.7 1.6 fusion.56
  333.3 1.5 convolution_convert_fusion.6
  334.8 6.4 %all-to-all-done.1 = bf16[4,16,32,256]{3,2,0,1:T(8,128)(2,1)} async-done(((bf16[4,16,32,256]{3,2,0,1:T(8,128)(2,1)}), bf16[4,16,32,256]{3,2,0,1:T(8,128)(2,1)}, u32[]{:S(2)}, u32[]{:S(2)}) %all-to-all-start.1) | async-done | bytes 1048608 | tf_op jit(solution)/shard_map/all_to_all | solution.py:1077
  341.2 4.4 all-to-all-start.5
  345.6 0.9 subtract_convert_fusion
  346.8 2.0 convolution_convert_fusion.1
  348.8 2.3 copy.113
  351.1 13.8 %all-to-all-done.5 = bf16[16,128,256]{2,1,0:T(8,128)(2,1)} async-done(((bf16[16,128,256]{2,1,0:T(8,128)(2,1)}), bf16[16,128,256]{2,1,0:T(8,128)(2,1)}, u32[]{:S(2)}, u32[]{:S(2)}) %all-to-all-start.5) | async-done | bytes 1048608 | tf_op jit(solution)/shard_map/all_to_all | solution.py:1126
  364.9 4.5 all-to-all-start.2
  369.8 2.2 fusion.91
  372.1 1.1 fusion.25
  373.5 1.4 fusion.35.lat_ref
  375.6 25.8 %back_input.1 = (f32[256,256]{1,0:T(8,128)S(1)}, bf16[16,2048]{1,0:T(8,128)(2,1)S(1)}) custom-call(bf16[256,2048]{1,0:T(8,128)(2,1)S(1)} %convolution_convert_fusion.5.part_ref, f32[256,256]{1,0:T(8,128)S(1)} %fusion.35.lat_ref, bf16[256,256]{1,0:T(8,128)(2,1)S(1)} %fusion.27.in_ref.x_ref, f32[256,1]{1,0:T(8,128)S(1)} %copy.124.inv_ref, ...), custom_call_target="tpu_custom_call" | custom-call | tf_op jit(solution)/shard_map/back_input/pallas_call | solution.py:340
  401.5 0.9 fusion.18
  402.4 2.0 copy.144
  404.4 7.0 %all-to-all-start.3 = ((bf16[16,128,576]{1,2,0:T(8,128)(2,1)}), bf16[16,128,576]{1,2,0:T(8,128)(2,1)S(1)}, u32[]{:S(2)}, u32[]{:S(2)}) async-start(bf16[16,128,576]{1,2,0:T(8,128)(2,1)} %bitcast.103), calls=%async_computation.4 | async-start | bytes 4718592 | tf_op jit(solution)/shard_map/all_to_all | solution.py:1126
  411.5 52.4 %ag_expert.3 = (bf16[4,4,288,128]{3,2,1,0:T(8,128)(2,1)S(1)}, bf16[4,4,288,128]{3,2,1,0:T(8,128)(2,1)S(1)}) custom-call(bf16[288,128]{1,0:T(8,128)(2,1)S(1)} %get-tuple-element.154.a_ref, bf16[288,128]{1,0:T(8,128)(2,1)S(1)} %get-tuple-element.153.b_ref), custom_call_target="tpu_custom_call" | custom-call | tf_op jit(solution)/shard_map/ag_expert/pallas_call | solution.py:474
  463.9 1.1 slice.152
  465.0 1.1 slice.153
  466.8 2.4 fusion.29
  469.2 1.1 fusion.30
  471.0 1.3 dynamic_slice.20
  473.5 1.4 convert_reduce_fusion.2
  475.7 2.5 convert_reduce_fusion.1
  478.1 1.0 convert_reduce_fusion
  479.2 1.1 copy.136
  481.8 8.6 %all-gather.8.cloned.1.call-done = bf16[4096,256]{1,0:T(8,128)(2,1)} async-done(((bf16[256,256]{1,0:T(8,128)(2,1)}), bf16[4096,256]{1,0:T(8,128)(2,1)}) %all-gather.8.cloned.1.call-update) | async-done | bytes 2097168 | tf_op jit(solution)/shard_map/all_gather | solution.py:1086
  490.4 3.0 fusion.26
  493.4 6.0 %copy.150 = f32[4,2048,176]{1,2,0:T(8,128)} copy(f32[4,2048,176]{1,2,0:T(8,128)} %bitcast.118) | data formatting | bytes 11534336
  499.4 6.0 %copy.151 = f32[4,2048,176]{1,2,0:T(8,128)} copy(f32[4,2048,176]{1,2,0:T(8,128)} %bitcast.117) | data formatting | bytes 11534336
  505.4 2.5 copy.152
  (258 shorter events, 23.0 us)
Async XLA Ops:
  7.2 76.1 %copy-start = (bf16[512,512]{1,0:T(8,128)(2,1)S(1)}, bf16[512,512]{1,0:T(8,128)(2,1)}, u32[]{:S(2)}) copy-start(bf16[512,512]{1,0:T(8,128)(2,1)} %param.25) | copy-start | bytes 1572868
  7.2 131.4 %all-gather.4.cloned.1.call-start = ((), (), s32[]{:S(2)}) async-start(), calls=%async_computation.8 | async-start | bytes 1179648 | tf_op jit(solution)/shard_map/all_gather | solution.py:968
  11.7 75.6 %copy-start.57 = (f32[256]{0:T(256)}, f32[256]{0:T(256)S(1)}, u32[]{:S(2)}) copy-start(f32[256]{0:T(256)S(1)} %get-tuple-element.167) | copy-start | bytes 3076
  41.2 1.5 copy-start.63
  41.2 1.5 copy-start.64
  42.6 2.8 copy-start.34
  42.6 96.0 %all-gather.6.cloned.1.call-start = ((), (), s32[]{:S(2)}) async-start(), calls=%async_computation.9 | async-start | bytes 9437184 | tf_op jit(solution)/shard_map/all_gather | solution.py:994
  66.8 247.4 %reduce-scatter.5.cloned.1.call-start = ((), (), s32[]{:S(2)}) async-start(), calls=%async_computation.10 | async-start | bytes 9437184 | tf_op jit(solution)/shard_map/reduce_scatter | solution.py:1076
  66.9 15.1 %copy-start.66 = (bf16[2048]{0:T(1024)(128)(2,1)S(1)}, bf16[2048]{0:T(1024)(128)(2,1)}, u32[]{:S(2)}) copy-start(bf16[2048]{0:T(1024)(128)(2,1)} %param.21) | copy-start | bytes 12292
  66.9 15.1 %copy-start.69 = (bf16[512]{0:T(512)(128)(2,1)S(1)}, bf16[512]{0:T(512)(128)(2,1)}, u32[]{:S(2)}) copy-start(bf16[512]{0:T(512)(128)(2,1)} %param.24) | copy-start | bytes 3076
  66.9 15.4 %copy-start.73 = (bf16[2048,576]{0,1:T(8,128)(2,1)S(1)}, bf16[2048,576]{0,1:T(8,128)(2,1)}, u32[]{:S(2)}) copy-start(bf16[2048,576]{0,1:T(8,128)(2,1)} %param.23) | copy-start | bytes 7077892
  81.9 2.0 copy-start.1
  82.0 2.0 copy-start.49
  82.0 191.8 %copy-start.47 = (f32[512]{0:T(512)}, f32[512]{0:T(512)S(1)}, u32[]{:S(2)}) copy-start(f32[512]{0:T(512)S(1)} %convert_element_type.199) | copy-start | bytes 6148
  82.3 186.4 %copy-start.61 = (f32[256]{0:T(256)}, f32[256]{0:T(256)S(1)}, u32[]{:S(2)}) copy-start(f32[256]{0:T(256)S(1)} %add_rsqrt_fusion) | copy-start | bytes 3076
  83.2 4.1 copy-start.14
  83.3 3.0 copy-start.59
  83.3 190.5 %copy-start.55 = (f32[256]{0:T(256)}, f32[256]{0:T(256)S(1)}, u32[]{:S(2)}) copy-start(f32[256]{0:T(256)S(1)} %fusion.66) | copy-start | bytes 3076
  83.9 4.9 copy-start.32
  86.3 2.6 copy-start.42
  87.1 3.7 copy-start.11
  87.2 3.1 copy-start.67
  87.6 2.8 copy-start.46
  87.6 2.7 copy-start.51
  87.6 2.7 copy-start.53
  87.7 2.7 copy-start.36
  87.7 2.7 copy-start.17
  90.4 43.8 %copy-start.29 = (bf16[2,128,256]{2,1,0:T(8,128)(2,1)}, bf16[2,128,256]{2,1,0:T(8,128)(2,1)S(1)}, u32[]{:S(2)}) copy-start(bf16[2,128,256]{2,1,0:T(8,128)(2,1)S(1)} %convolution_convert_fusion.10) | copy-start | bytes 393220
  256.7 1.8 copy-start.39
  256.7 222.4 %reduce-scatter.7.cloned.1.call-start = ((), (), s32[]{:S(2)}) async-start(), calls=%async_computation.12 | async-start | bytes 5013504
  268.6 1.9 copy-start.18
  268.6 1.9 copy-start.20
  272.2 1.7 copy-start.15
  275.0 41.5 %all-to-all-start.4 = ((bf16[16,32,512]{2,1,0:T(8,128)(2,1)}), bf16[16,32,512]{2,1,0:T(8,128)(2,1)S(1)}, u32[]{:S(2)}, u32[]{:S(2)}) async-start(bf16[16,32,512]{2,1,0:T(8,128)(2,1)} %bitcast.38), calls=%async_computation.5 | async-start | bytes 1048576 | tf_op jit(solution)/shard_map/all_to_all | solution.py:1126
  316.6 6.8 %copy-start.23 = (bf16[16,32,512]{2,1,0:T(8,128)(2,1)}, bf16[16,32,512]{2,1,0:T(8,128)(2,1)S(1)}, u32[]{:S(2)}) copy-start(bf16[16,32,512]{2,1,0:T(8,128)(2,1)S(1)} %all-to-all-done.4) | copy-start | bytes 1572868
  316.6 24.6 %all-to-all-start.1 = ((bf16[4,16,32,256]{3,2,0,1:T(8,128)(2,1)}), bf16[4,16,32,256]{3,2,0,1:T(8,128)(2,1)}, u32[]{:S(2)}, u32[]{:S(2)}) async-start(bf16[4,16,32,256]{3,2,0,1:T(8,128)(2,1)} %copy.112), calls=%async_computation.2 | async-start | bytes 2097152 | tf_op jit(solution)/shard_map/all_to_all | solution.py:1077
  324.2 7.4 %copy-start.58 = (f32[256]{0:T(256)S(1)}, f32[256]{0:T(256)}, u32[]{:S(2)}) copy-start(f32[256]{0:T(256)} %copy-done.57) | copy-start | bytes 3076
  324.3 7.4 %copy-start.68 = (f32[32]{0:T(128)S(1)}, f32[32]{0:T(128)}, u32[]{:S(2)}) copy-start(f32[32]{0:T(128)} %copy-done.67) | copy-start | bytes 388
  324.3 9.0 %copy-start.21 = (bf16[256,2048]{1,0:T(8,128)(2,1)S(1)}, bf16[256,2048]{1,0:T(8,128)(2,1)}, u32[]{:S(2)}) copy-start(bf16[256,2048]{1,0:T(8,128)(2,1)} %get-tuple-element.44) | copy-start | bytes 3145732
  324.3 9.0 %copy-start.30 = (bf16[2,128,256]{2,1,0:T(8,128)(2,1)S(1)}, bf16[2,128,256]{2,1,0:T(8,128)(2,1)}, u32[]{:S(2)}) copy-start(bf16[2,128,256]{2,1,0:T(8,128)(2,1)} %copy-done.29) | copy-start | bytes 393220
  333.3 13.2 %copy-start.48 = (f32[512]{0:T(512)S(1)}, f32[512]{0:T(512)}, u32[]{:S(2)}) copy-start(f32[512]{0:T(512)} %copy-done.47) | copy-start | bytes 6148
  333.3 13.2 %copy-start.56 = (f32[256]{0:T(256)S(1)}, f32[256]{0:T(256)}, u32[]{:S(2)}) copy-start(f32[256]{0:T(256)} %copy-done.55) | copy-start | bytes 3076
  334.8 12.0 %copy-start.60 = (f32[256]{0:T(256)S(1)}, f32[256]{0:T(256)}, u32[]{:S(2)}) copy-start(f32[256]{0:T(256)} %copy-done.59) | copy-start | bytes 3076
  334.8 12.0 %copy-start.2 = (bf16[256,2048]{1,0:T(8,128)(2,1)S(1)}, bf16[256,2048]{1,0:T(8,128)(2,1)}, u32[]{:S(2)}) copy-start(bf16[256,2048]{1,0:T(8,128)(2,1)} %copy-done.1) | copy-start | bytes 3145732
  334.8 12.0 %copy-start.50 = (f32[2048]{0:T(1024)S(1)}, f32[2048]{0:T(1024)}, u32[]{:S(2)}) copy-start(f32[2048]{0:T(1024)} %copy-done.49) | copy-start | bytes 24580
  334.8 12.0 %copy-start.62 = (f32[256]{0:T(256)S(1)}, f32[256]{0:T(256)}, u32[]{:S(2)}) copy-start(f32[256]{0:T(256)} %copy-done.61) | copy-start | bytes 3076
  341.2 23.7 %all-to-all-start.5 = ((bf16[16,128,256]{2,1,0:T(8,128)(2,1)}), bf16[16,128,256]{2,1,0:T(8,128)(2,1)}, u32[]{:S(2)}, u32[]{:S(2)}) async-start(bf16[16,128,256]{2,1,0:T(8,128)(2,1)} %bitcast.122), calls=%async_computation.6 | async-start | bytes 2097152 | tf_op jit(solution)/shard_map/all_to_all | solution.py:1126
  364.9 7.1 %copy-start.6 = (f32[256,256]{1,0:T(8,128)S(1)}, f32[256,256]{1,0:T(8,128)}, u32[]{:S(2)}) copy-start(f32[256,256]{1,0:T(8,128)} %copy-done.5) | copy-start | bytes 786436
  364.9 39.5 %all-to-all-start.2 = ((bf16[16,128,384]{2,1,0:T(8,128)(2,1)}), bf16[16,128,384]{2,1,0:T(8,128)(2,1)}, u32[]{:S(2)}, u32[]{:S(2)}) async-start(bf16[16,128,384]{2,1,0:T(8,128)(2,1)} %bitcast.125), calls=%async_computation.3 | async-start | bytes 3145728 | tf_op jit(solution)/shard_map/all_to_all | solution.py:1126
  369.4 120.9 %all-gather.8.cloned.1.call-start = ((), (), s32[]{:S(2)}) async-start(), calls=%async_computation.11 | async-start | bytes 2228224 | tf_op jit(solution)/shard_map/all_gather | solution.py:1086
  369.7 2.3 copy-start.16
  369.8 2.3 copy-start.19
  369.8 2.3 copy-start.35
  373.2 1.6 copy-start.25
  373.4 2.2 copy-start.7
  373.4 2.2 copy-start.10
  404.4 7.0 %copy-start.65 = (bf16[288]{0:T(512)(128)(2,1)S(1)}, bf16[288]{0:T(512)(128)(2,1)}, u32[]{:S(2)}) copy-start(bf16[288]{0:T(512)(128)(2,1)} %pad.10.clone) | copy-start | bytes 1732
  404.4 73.7 %all-to-all-start.3 = ((bf16[16,128,576]{1,2,0:T(8,128)(2,1)}), bf16[16,128,576]{1,2,0:T(8,128)(2,1)S(1)}, u32[]{:S(2)}, u32[]{:S(2)}) async-start(bf16[16,128,576]{1,2,0:T(8,128)(2,1)} %bitcast.103), calls=%async_computation.4 | async-start | bytes 4718592 | tf_op jit(solution)/shard_map/all_to_all | solution.py:1126
  463.9 2.9 copy-start.70
  466.7 2.4 copy-start.27
  469.1 3.7 copy-start.24
  478.1 12.2 %copy-start.71 = (s32[256]{0:T(256)S(1)}, s32[256]{0:T(256)}, u32[]{:S(2)}) copy-start(s32[256]{0:T(256)} %fusion.63) | copy-start | bytes 3076
  493.4 12.0 %slice-start = ((s8[5767168]{0:T(1024)(128)(4,1)}), s8[4194304]{0:T(1024)(128)(4,1)S(1)}, s32[]{:S(2)}) async-start(s8[5767168]{0:T(1024)(128)(4,1)} %bitcast.115), calls=%async_computation.13 | async-start | bytes 8388608
  499.4 6.0 %slice-start.1 = ((s8[5767168]{0:T(1024)(128)(4,1)}), s8[1572864]{0:T(1024)(128)(4,1)S(1)}, s32[]{:S(2)}) async-start(s8[5767168]{0:T(1024)(128)(4,1)} %bitcast.115), calls=%async_computation.14 | async-start | bytes 3145728
  (22 other events, 22.8 us)
Sparse Core Ops, SparseCore 0:
  42.7 24.5 all-gather.3
  69.6 67.3 all-gather.5
  256.9 57.3 reduce-scatter.4
  318.0 124.9 reduce-scatter.6
  445.6 44.7 all-gather.7
